TPU v7x, 32 devices: a whole 2x2x4 slice. The times are simulated.
32 devices in a mesh: fsdp: 8 (over y, x, core), dp: 4 (over z).
Axes of the slice: x: 2, y: 2, z: 4, core: 2. Of those that a mesh axis runs over, the one named last changes fastest.
Arguments:
- grad_out: bfloat16 [4096, 8192], P('dp', 'fsdp'), may hold values from -6 to 6
- inputs: bfloat16 [4096, 8192], P('dp', 'fsdp'), may hold values from -6 to 6
- gate_pre: bfloat16 [4096, 28672], P('dp', 'fsdp'), may hold values from -8 to 8
- down_weight: bfloat16 [28672, 8192], P('fsdp', 'dp'), may hold values from -0.0625 to 0.0625
- input_adapter_factor: bfloat16 [8192, 128], P('fsdp'), may hold values from -0.0625 to 0.0625
- adapter_second: bfloat16 [128, 28672], P(None, 'fsdp'), may hold values from -0.03125 to 0.03125
- sketch_model: int32 [8192, 64], P('fsdp'), may hold values from -1 to 1, as said below
- sketch_hidden: int32 [28672, 64], P('fsdp'), may hold values from -1 to 1, as said below
- mixer_first: int32 [128, 128], replicated, may hold values from -1 to 1, as said below
- second_sign_mixer: int32 [128, 128], replicated, may hold values from -1 to 1, as said below
Outputs:
- features: float32 [16, 8192], P('dp')
- scores: float32 [16], P('dp')
Inputs may be any that keep to these rules, and one draw needn't show every extreme that they name: `sketch_model`: every entry is -1 or +1. `sketch_hidden`: every entry is -1 or +1. `mixer_first`: every entry is -1 or +1. `second_sign_mixer`: every entry is -1 or +1.
All inputs are finite; a program needn't handle non-finite values.
Results may differ from a plain program's by a relative error of at most 0.0039.
Values may be sent and summed in bfloat16 or wider, within the bound.
A program may use at most 256 MiB of HBM per device.

v0:
```python
import jax
import jax.numpy as jnp
from jax import lax
from jax.sharding import PartitionSpec as P

K1 = 64
K2 = 128
SEQ = 256


def contract_last(left, right):
    return lax.dot_general(
        left, right, (((1,), (1,)), ((), ())), preferred_element_type=jnp.float32
    )


def body(
    grad_out,
    inputs,
    gate_pre,
    down_weight,
    input_adapter_factor,
    adapter_second,
    sketch_model,
    sketch_hidden,
    mixer_first,
    second_sign_mixer,
):
    weights = lax.all_gather(down_weight, "dp", axis=1, tiled=True)
    tokens = grad_out.shape[0]
    gathered = lax.all_gather(grad_out, "fsdp", axis=1, tiled=True)
    upstream = contract_last(gathered, weights)
    scaled_result = (upstream * jax.nn.silu(gate_pre.astype(jnp.float32))).astype(jnp.bfloat16)
    low_rank_piece = jnp.dot(inputs, input_adapter_factor, preferred_element_type=jnp.float32)
    sketch_part = jnp.dot(
        inputs, sketch_model.astype(jnp.bfloat16), preferred_element_type=jnp.float32
    )
    back_part = contract_last(scaled_result, adapter_second)
    sign_mixer_float = mixer_first.astype(jnp.float32)
    low_rank_input = lax.psum(low_rank_piece, "fsdp").astype(jnp.bfloat16)
    back_full = lax.psum(back_part, "fsdp")
    right_first = jnp.dot(back_full, sign_mixer_float, precision=lax.Precision.HIGHEST)
    left_model = sketch_part
    second_right_factor = jnp.dot(
        low_rank_input, second_sign_mixer.astype(jnp.bfloat16), preferred_element_type=jnp.float32
    )
    left_hidden = jnp.dot(
        scaled_result, sketch_hidden.astype(jnp.bfloat16), preferred_element_type=jnp.float32
    )
    count = tokens // SEQ
    left_model = left_model.reshape(count, SEQ, K1)
    left_hidden = left_hidden.reshape(count, SEQ, K1)
    right_first = right_first.reshape(count, SEQ, K2)
    second_right_factor = second_right_factor.reshape(count, SEQ, K2)
    partial_proj = jnp.einsum(
        "esa,esb->eab", left_hidden, second_right_factor, precision=lax.Precision.HIGHEST
    )
    partial_proj = partial_proj + jnp.einsum(
        "esa,esb->eab", left_model, right_first, precision=lax.Precision.HIGHEST
    )
    projected = lax.psum(partial_proj, "fsdp").reshape(count, K1 * K2)
    features = projected * lax.rsqrt(jnp.mean(projected * projected, axis=1, keepdims=True) + 1e-06)
    summed_result = lax.psum(jnp.sum(features, axis=0), "dp")
    centre = summed_result / (count * lax.axis_size("dp"))
    scores = jnp.dot(features, centre, precision=lax.Precision.HIGHEST) / (
        K1 * K2 * jnp.sqrt(jnp.mean(centre * centre) + 1e-06)
    )
    return (features, scores)


def solution(mesh):
    placed = (
        P("dp", "fsdp"),
        P("dp", "fsdp"),
        P("dp", "fsdp"),
        P("fsdp", "dp"),
        P("fsdp", None),
        P(None, "fsdp"),
        P("fsdp", None),
        P("fsdp", None),
        P(),
        P(),
    )
    return jax.shard_map(
        body, mesh=mesh, in_specs=placed, out_specs=(P("dp", None), P("dp")), check_vma=False
    )
```

profile of v0, /device:TPU:0, one launch (start us, length us, event | category | flops | bytes accessed | tf_op | source)
XLA Modules:
  0.0 1303.8 jit_solution(11398896230159215997)
XLA Ops:
  7.2 0.0 copy-start
  7.2 0.0 copy-start.3
  7.2 0.0 copy-start.6
  7.2 0.0 copy-start.2
  7.2 0.0 all-gather.3.cloned.1.call-start
  7.3 0.7 all-gather.3.cloned.1.call-update
  7.9 0.0 all-gather.5.cloned.1.call-start
  8.0 0.7 all-gather.5.cloned.1.call-update
  8.7 0.0 all-reduce.4.cloned.1.call-start
  8.7 0.0 copy-done
  8.8 0.0 copy-done.3
  8.8 0.7 fusion.20
  9.5 41.0 %all-reduce.7 = bf16[1024,128]{1,0:T(8,128)(2,1)S(1)} all-reduce(f32[1024,128]{1,0:T(8,128)S(1)} %fusion.20), channel_id=1, replica_groups=mesh['fsdp'=8,'dp'=4] {'fsdp'}, use_global_device_ids=true, to_apply=%region_0.1 | all-reduce | flops 131072 | bytes 786432 | tf_op jit(solution)/shard_map/psum | solution.py:40
  50.5 0.0 copy-done.6
  50.5 0.2 fusion.13
  50.7 0.0 copy-done.2
  50.7 0.8 fusion.15
  51.4 56.7 %all-gather.3.cloned.1.call-done = bf16[1024,8192]{1,0:T(8,128)(2,1)} async-done(((bf16[1024,1024]{1,0:T(8,128)(2,1)}), bf16[1024,8192]{1,0:T(8,128)(2,1)}) %all-gather.3.cloned.1.call-update) | async-done | bytes 16777232 | tf_op jit(solution)/shard_map/all_gather | solution.py:31
  108.2 976.0 %all-gather.5.cloned.1.call-done = bf16[3584,8192]{1,0:T(8,128)(2,1)} async-done(((bf16[3584,2048]{1,0:T(8,128)(2,1)}), bf16[3584,8192]{1,0:T(8,128)(2,1)}) %all-gather.5.cloned.1.call-update) | async-done | bytes 58720272 | tf_op jit(solution)/shard_map/all_gather | solution.py:29
  1084.2 0.0 copy-start.1
  1084.2 73.4 %fusion.4 = bf16[1024,3584]{1,0:T(8,128)(2,1)} fusion(bf16[1024,3584]{1,0:T(8,128)(2,1)} %param.12, bf16[1024,8192]{1,0:T(8,128)(2,1)} %all-gather.3.cloned.1.call-done, bf16[3584,8192]{1,0:T(8,128)(2,1)} %all-gather.5.cloned.1.call-done), kind=kOutput, calls=%fused_computation.6 | convolution fusion | flops 60155232256 | bytes 90177536 | tf_op jit(solution)/shard_map/dot_general | solution.py:12
  1157.5 0.0 copy-start.5
  1157.5 6.2 fusion.21
  1163.7 0.0 all-reduce.4.cloned.1.call-update
  1163.7 0.2 all-reduce.6.cloned.1.call-start
  1164.0 5.6 fusion.6
  1169.5 0.5 fusion.10
  1170.0 46.6 %all-reduce.4.cloned.1.call-done = f32[1024,128]{1,0:T(8,128)} async-done(((f32[1024,128]{1,0:T(8,128)}), f32[1024,128]{1,0:T(8,128)}) %all-reduce.4.cloned.1.call-update) | async-done | bytes 524304 | tf_op jit(solution)/shard_map/psum | solution.py:41
  1216.6 0.0 copy-done.5
  1216.6 1.6 fusion.17
  1218.2 1.1 convolution_add_fusion
  1219.3 0.0 all-reduce.6.cloned.1.call-update
  1219.4 53.3 %all-reduce.6.cloned.1.call-done = f32[4,64,128]{2,1,0:T(8,128)} async-done(((f32[4,64,128]{2,1,0:T(8,128)}), f32[4,64,128]{2,1,0:T(8,128)}) %all-reduce.6.cloned.1.call-update) | async-done | bytes 131088 | tf_op jit(solution)/shard_map/psum | solution.py:61
  1272.6 1.0 multiply_reduce_fusion.1
  1273.7 1.0 bitcast_multiply_fusion
  1274.7 0.0 copy-start.4
  1274.7 1.0 multiply_reduce_fusion
  1275.7 19.0 %psum.31 = f32[8192]{0:T(1024)S(1)} all-reduce(f32[8192]{0:T(1024)S(1)} %bitcast.38), channel_id=1, replica_groups=mesh['fsdp'=8,'dp'=4] {'dp'}, use_global_device_ids=true, to_apply=%region_5.6 | all-reduce | flops 8192 | bytes 65536 | tf_op jit(solution)/shard_map/psum | solution.py:63
  1294.7 0.6 multiply_reduce_fusion.2
  1296.0 1.2 fusion.5
  1297.2 0.0 copy-done.4
  1297.2 0.0 copy-done.1
  (1 shorter events, 0.0 us)
Async XLA Ops:
  7.2 1.6 copy-start
  7.2 1.6 copy-start.3
  7.2 43.3 %copy-start.6 = (s32[128,128]{1,0:T(8,128)S(1)}, s32[128,128]{1,0:T(8,128)}, u32[]{:S(2)}) copy-start(s32[128,128]{1,0:T(8,128)} %param.19) | copy-start | bytes 196612
  7.2 43.5 %copy-start.2 = (s32[1024,64]{0,1:T(8,128)S(1)}, s32[1024,64]{0,1:T(8,128)}, u32[]{:S(2)}) copy-start(s32[1024,64]{0,1:T(8,128)} %param.16) | copy-start | bytes 786436
  7.2 100.9 %all-gather.3.cloned.1.call-start = ((), (), s32[]{:S(2)}) async-start(), calls=%async_computation | async-start | bytes 18874368 | tf_op jit(solution)/shard_map/all_gather | solution.py:31
  7.9 1076.2 %all-gather.5.cloned.1.call-start = ((), (), s32[]{:S(2)}) async-start(), calls=%async_computation.1 | async-start | bytes 73400320 | tf_op jit(solution)/shard_map/all_gather | solution.py:29
  8.7 1207.9 %all-reduce.4.cloned.1.call-start = ((), (), s32[]{:S(2)}) async-start(), calls=%async_computation.2 | async-start | bytes 1048576 | tf_op jit(solution)/shard_map/psum | solution.py:41
  1084.2 213.0 %copy-start.1 = (bf16[1024,1024]{1,0:T(8,128)(2,1)S(1)}, bf16[1024,1024]{1,0:T(8,128)(2,1)}, u32[]{:S(2)}) copy-start(bf16[1024,1024]{1,0:T(8,128)(2,1)} %param.11) | copy-start | bytes 6291460
  1157.5 59.1 %copy-start.5 = (s32[128,128]{1,0:T(8,128)S(1)}, s32[128,128]{1,0:T(8,128)}, u32[]{:S(2)}) copy-start(s32[128,128]{1,0:T(8,128)} %param.18) | copy-start | bytes 196612
  1163.7 108.9 %all-reduce.6.cloned.1.call-start = ((), (), s32[]{:S(2)}) async-start(), calls=%async_computation.3 | async-start | bytes 262144 | tf_op jit(solution)/shard_map/psum | solution.py:61
  1274.7 22.5 %copy-start.4 = (f32[4,8192]{1,0:T(4,128)}, f32[4,8192]{1,0:T(4,128)S(1)}, u32[]{:S(2)}) copy-start(f32[4,8192]{1,0:T(4,128)S(1)} %bitcast_multiply_fusion) | copy-start | bytes 393220
Sparse Core Ops, SparseCore 0:
  10.0 98.1 all-gather.2
  109.7 974.3 all-gather.4
  1163.9 52.7 all-reduce.3
  1220.4 52.2 all-reduce.5
where the time goes:
time: 1300 us
  waiting for transfers between devices  1130 us (87%)
  matrix products  91.2 us (7%)
  blocking collectives  60 us (5%)
  between operations  14.6 us (1%)
    all_gather x1, waiting for transfers between devices, body(): weights = lax.all_gather(down_weight, 'dp', axis=1, tiled=True)  976 us
    dot_general x2, matrix products, contract_last(): lax.dot_general(left, right, (((1,), (1,)), ((), ())), preferred_element_...  79.5 us
    all_gather x1, waiting for transfers between devices, body(): gathered = lax.all_gather(grad_out, 'fsdp', axis=1, tiled=True)  56.7 us
    psum x1, waiting for transfers between devices, body(): projected = lax.psum(partial_proj, 'fsdp').reshape(count, K1 * K2)  53.3 us
    psum x1, waiting for transfers between devices, body(): back_full = lax.psum(back_part, 'fsdp')  46.6 us
    psum x1, blocking collectives, body(): low_rank_input = lax.psum(low_rank_piece, 'fsdp').astype(jnp.bfloat16)  41 us
  transfers between devices with their start and end apart: 4, of which 4 were waited for; matrix products, arithmetic and copies ran while one was open for 1% of the time, Pallas kernels for 0%

commit v1 on v0

v1 whole, which is shorter than its diff:
```python
import jax
import jax.numpy as jnp
from jax import lax
from jax.sharding import PartitionSpec as P

K1 = 64
K2 = 128
SEQ = 256
CHUNKS = 14
LAG = 2
GROUP = 2


def contract_last(left, right):
    return lax.dot_general(
        left, right, (((1,), (1,)), ((), ())), preferred_element_type=jnp.float32
    )


def body(
    grad_out,
    inputs,
    gate_pre,
    down_weight,
    input_adapter_factor,
    adapter_second,
    sketch_model,
    sketch_hidden,
    mixer_first,
    second_sign_mixer,
):
    z = lax.axis_index("dp")
    planes = lax.axis_size("dp")
    ranks = lax.axis_size("fsdp")
    outer = (z == 0) | (z == 3)
    low = z < 2
    tokens, hidden = gate_pre.shape
    width = hidden // CHUNKS
    span = width * GROUP
    rank = adapter_second.shape[0]

    own = [gate_pre[:, i * width : (i + 1) * width] for i in range(CHUNKS)]

    rows = lax.all_to_all(grad_out, "fsdp", 0, 1, tiled=True)
    rows = lax.all_to_all(rows, "dp", 1, 0, tiled=True)
    rows = rows.reshape(planes, tokens // ranks, down_weight.shape[1])

    def gathered(block):
        piece = lax.dynamic_index_in_dim(rows, block, 0, keepdims=False)
        return lax.all_gather(piece, "fsdp", axis=0, tiled=True)

    block_a = z ^ 1
    block_c = jnp.where(low, 2, 1)
    block_d = jnp.where(low, 3, 0)
    grad_a = gathered(block_a)
    grad_c = gathered(block_c)
    grad_b = gathered(z)
    grad_d = gathered(block_d)

    model_factors = jnp.concatenate(
        [input_adapter_factor, sketch_model.astype(jnp.bfloat16)], axis=1
    )
    model_side = jnp.dot(inputs, model_factors, preferred_element_type=jnp.float32)
    model_side = lax.psum(model_side, "fsdp")
    second_right = jnp.dot(
        model_side[:, :rank].astype(jnp.bfloat16),
        second_sign_mixer.astype(jnp.bfloat16),
        preferred_element_type=jnp.float32,
    )
    model_side = jnp.concatenate([second_right, model_side[:, rank:]], axis=1)
    model_side = lax.all_gather(model_side, "dp", axis=0, tiled=True)

    hidden_factors = jnp.concatenate(
        [adapter_second, sketch_hidden.astype(jnp.bfloat16).T], axis=0
    )

    def silu(v):
        return jax.nn.silu(v.astype(jnp.float32))

    def upstream(grad, group):
        return contract_last(grad, down_weight[group * span : (group + 1) * span])

    def sketched(scaled, group):
        return contract_last(scaled, hidden_factors[:, group * span : (group + 1) * span])

    def joined(pieces):
        return jnp.concatenate(pieces, axis=1)

    steps = 2 * CHUNKS + LAG
    from_left, from_right = [], []
    partial_out = [None] * CHUNKS
    total_a = total_b = total_c = total_d = 0.0

    def near(s):
        return jnp.where(low, from_left[s], from_right[s])

    def far(s):
        ahead = jnp.where(low, from_right[s], from_left[s])
        late = jnp.where(low, from_right[s + LAG], from_left[s + LAG])
        return jnp.where(outer, late, ahead)

    def to_send(s, received, first, second, third):
        if s < CHUNKS:
            value = own[s]
        elif s < 2 * CHUNKS:
            value = jnp.where(z == first, partial_out[s - CHUNKS], received[s - CHUNKS])
        else:
            return received[s - LAG]
        if s >= LAG:
            value = jnp.where(z == third, received[s - LAG], value)
        return value

    for s in range(steps):
        if CHUNKS <= s < 2 * CHUNKS and s % GROUP == 0:
            group = (s - CHUNKS) // GROUP
            gate = joined([near(group * GROUP + k) for k in range(GROUP)])
            up = upstream(grad_a, group)
            scaled = jnp.where(outer, up, up * silu(gate)).astype(jnp.bfloat16)
            total_a = total_a + sketched(scaled, group)
            for k in range(GROUP):
                partial_out[group * GROUP + k] = scaled[:, k * width : (k + 1) * width]
        pairs = []
        if s < 2 * CHUNKS:
            pairs += [(0, 1), (1, 2)]
        if s >= LAG:
            pairs += [(2, 3)]
        going_right = to_send(s, from_left, 0, 1, 2)
        going_left = to_send(s, from_right, 3, 2, 1)
        from_left.append(lax.ppermute(going_right, "dp", pairs))
        from_right.append(lax.ppermute(going_left, "dp", [(3 - a, 3 - b) for a, b in pairs]))

    for group in range(CHUNKS // GROUP):
        places = [group * GROUP + k for k in range(GROUP)]
        scaled = (upstream(grad_c, group) * silu(joined([far(i) for i in places]))).astype(
            jnp.bfloat16
        )
        total_c = total_c + sketched(scaled, group)
        extra = joined([near(CHUNKS + i) for i in places]).astype(jnp.float32)
        up = upstream(grad_b, group) + jnp.where(outer, 0.0, extra)
        gate = gate_pre[:, group * span : (group + 1) * span]
        scaled = (up * silu(gate)).astype(jnp.bfloat16)
        total_b = total_b + sketched(scaled, group)
        scaled = (
            upstream(grad_d, group) * silu(joined([far(CHUNKS + i) for i in places]))
        ).astype(jnp.bfloat16)
        total_d = total_d + sketched(scaled, group)

    sums = jnp.zeros((planes, tokens, rank + K1), jnp.float32)
    for block, total in (
        (block_a, jnp.where(outer, 0.0, total_a)),
        (z, total_b),
        (block_c, total_c),
        (block_d, total_d),
    ):
        sums = lax.dynamic_update_index_in_dim(sums, total, block, 0)

    count = tokens // SEQ
    sums = sums.reshape(planes * count, SEQ, rank + K1)
    model_side = model_side.reshape(planes * count, SEQ, K2 + K1)
    back, left_hidden = sums[..., :rank], sums[..., rank:]
    second_right, left_model = model_side[..., :K2], model_side[..., K2:]
    projected = jnp.einsum(
        "esa,esb->eab", left_hidden, second_right, precision=lax.Precision.HIGHEST
    )
    crossed = jnp.einsum("esa,esr->ear", left_model, back, precision=lax.Precision.HIGHEST)
    projected = projected + jnp.einsum(
        "ear,rb->eab",
        crossed,
        mixer_first.astype(jnp.float32),
        precision=lax.Precision.HIGHEST,
    )
    projected = lax.psum(projected, ("fsdp", "dp")).reshape(planes * count, K1 * K2)
    features = projected * lax.rsqrt(jnp.mean(projected * projected, axis=1, keepdims=True) + 1e-06)
    centre = jnp.sum(features, axis=0) / (planes * count)
    features = lax.dynamic_slice_in_dim(features, z * count, count, 0)
    scores = jnp.dot(features, centre, precision=lax.Precision.HIGHEST) / (
        K1 * K2 * jnp.sqrt(jnp.mean(centre * centre) + 1e-06)
    )
    return (features, scores)


def solution(mesh):
    placed = (
        P("dp", "fsdp"),
        P("dp", "fsdp"),
        P("dp", "fsdp"),
        P("fsdp", "dp"),
        P("fsdp", None),
        P(None, "fsdp"),
        P("fsdp", None),
        P("fsdp", None),
        P(),
        P(),
    )
    return jax.shard_map(
        body, mesh=mesh, in_specs=placed, out_specs=(P("dp", None), P("dp")), check_vma=False
    )
```

time: 1300 us -> 1040 us (0.80); the launches traced: 1300 us -> 1030 us
  waiting for transfers between devices: 1130 us -> 418 us
  starting transfers between devices: 0.34 us -> 206 us
  matrix products: 91.2 us -> 206 us
  local copies, waits for them, and re-layouts: 0.06 us -> 98.7 us
  other arithmetic: 3.68 us -> 52.2 us
  blocking collectives: 60 us -> 32 us
    all_gather x2 -> x5, waiting for transfers between devices: 1030 us -> 0.06 us  [the longest x4 0.04 us: gathered(): return lax.all_gather(piece, 'fsdp', axis=0, tiled=True)]
    ppermute x0 -> x60, waiting for transfers between devices: none -> 239 us  [the longest x30 127 us: body(): from_left.append(lax.ppermute(going_right, 'dp', pairs))]
    ppermute x0 -> x60, starting transfers between devices: none -> 187 us  [the longest x30 149 us: body(): from_left.append(lax.ppermute(going_right, 'dp', pairs))]
    dot_general x2 -> x35, matrix products: 79.5 us -> 192 us  [contract_last(): lax.dot_general(left, right, (((1,), (1,)), ((), ())), preferred_element_...]
    dynamic_update_slice x0 -> x4, local copies, waits for them, and re-layouts: none -> 61 us  [body(): sums = lax.dynamic_update_index_in_dim(sums, total, block, 0)]
    psum x2 -> x0, blocking collectives: 60 us -> none  [the longest x1 41 us: body(): low_rank_input = lax.psum(low_rank_piece, 'fsdp').astype(jnp.bfloat16)]
    select_n x0 -> x22, other arithmetic: none -> 48 us  [the longest x19 34.1 us: to_send(): value = jnp.where(z == third, received[s - LAG], value)]
    all_to_all x0 -> x1, waiting for transfers between devices: none -> 45.5 us  [body(): rows = lax.all_to_all(rows, 'dp', 1, 0, tiled=True)]
  transfers between devices with their start and end apart: 4 -> 68, of which waited for: 4 -> 39; matrix products, arithmetic and copies ran while one was open for 1% -> 22% of each run, Pallas kernels for 0% -> 0%
where the time goes in v1:
time: 1040 us; the launch traced here: 1030 us
  waiting for transfers between devices  418 us (40%)
  starting transfers between devices  206 us (20%)
  matrix products  206 us (20%)
  local copies, waits for them, and re-layouts  98.7 us (9%)
  other arithmetic  52.2 us (5%)
  blocking collectives  32 us (3%)
  between operations  17.1 us (2%)
    dot_general x35, matrix products, contract_last(): lax.dot_general(left, right, (((1,), (1,)), ((), ())), preferred_element_...  192 us
    ppermute x30, starting transfers between devices, body(): from_left.append(lax.ppermute(going_right, 'dp', pairs))  149 us
    ppermute x30, waiting for transfers between devices, body(): from_left.append(lax.ppermute(going_right, 'dp', pairs))  127 us
    psum x1, waiting for transfers between devices, body(): lax.psum(projected, ('fsdp', 'dp')).reshape(planes * count, K1 * K2)  124 us
    ppermute x30, waiting for transfers between devices, body(): lax.ppermute(going_left, 'dp', [(3 - a, 3 - b) for a, b in pairs])  112 us
    dynamic_update_slice x4, local copies, waits for them, and re-layouts, body(): sums = lax.dynamic_update_index_in_dim(sums, total, block, 0)  61 us
    all_to_all x1, waiting for transfers between devices, body(): rows = lax.all_to_all(rows, 'dp', 1, 0, tiled=True)  45.5 us
    ppermute x30, starting transfers between devices, body(): lax.ppermute(going_left, 'dp', [(3 - a, 3 - b) for a, b in pairs])  38.5 us
  transfers between devices with their start and end apart: 68, of which 39 were waited for; matrix products, arithmetic and copies ran while one was open for 22% of the time, Pallas kernels for 0%

profile of v1, /device:TPU:0, one launch (start us, length us, event | category | flops | bytes accessed | tf_op | source)
XLA Modules:
  0.0 1029.6 jit_solution(8233027035292754576)
XLA Ops:
  7.2 32.0 %all_to_all.29 = bf16[8,128,1024]{2,1,0:T(8,128)(2,1)} all-to-all(bf16[8,128,1024]{2,1,0:T(8,128)(2,1)} %bitcast.242), channel_id=1, replica_groups=mesh['fsdp'=8,'dp'=4] {'fsdp'}, dimensions={0} | all-to-all | bytes 4194304 | tf_op jit(solution)/shard_map/all_to_all | solution.py:44
  43.1 5.5 all-to-all-start.1
  50.8 45.5 %all-to-all-done.1 = bf16[128,4,2048]{0,2,1:T(8,128)(2,1)} async-done(((bf16[128,4,2048]{0,2,1:T(8,128)(2,1)}), bf16[128,4,2048]{0,2,1:T(8,128)(2,1)}, u32[]{:S(2)}, u32[]{:S(2)}) %all-to-all-start.1) | async-done | bytes 2097184 | tf_op jit(solution)/shard_map/all_to_all | solution.py:45
  99.3 8.5 all-reduce.3.cloned.1.call-done
  124.3 6.8 collective-permute-done
  131.0 9.1 collective-permute-done.2
  153.7 9.8 collective-permute-done.4
  163.6 8.3 collective-permute-done.5
  171.9 11.2 %collective-permute-done.6 = bf16[1024,256]{1,0:T(8,128)(2,1)S(1)} collective-permute-done((bf16[1024,256]{1,0:T(8,128)(2,1)}, bf16[1024,256]{1,0:T(8,128)(2,1)S(1)}, u32[]{:S(2)}, u32[]{:S(2)}) %collective-permute-start.6) | collective-permute-done | bytes 524320 | tf_op jit(solution)/shard_map/ppermute | solution.py:129
  186.0 19.5 %collective-permute-start.10 = (bf16[1024,256]{1,0:T(8,128)(2,1)S(1)}, bf16[1024,256]{1,0:T(8,128)(2,1)S(1)}, u32[]{:S(2)}, u32[]{:S(2)}) collective-permute-start(bf16[1024,256]{1,0:T(8,128)(2,1)S(1)} %get-tuple-element.16), channel_id=1, source_target_pairs={{0,1},{1,2},{2,3},{4,5},{5,6},{6,7},{8,9},{9,10},{10,11},{12,13},{... | collective-permute-start | bytes 1572872 | tf_op jit(solution)/shard_map/ppermute | solution.py:129
  212.1 16.1 %collective-permute-done.10 = bf16[1024,256]{1,0:T(8,128)(2,1)S(1)} collective-permute-done((bf16[1024,256]{1,0:T(8,128)(2,1)S(1)}, bf16[1024,256]{1,0:T(8,128)(2,1)S(1)}, u32[]{:S(2)}, u32[]{:S(2)}) %collective-permute-start.10) | collective-permute-done | bytes 524320 | tf_op jit(solution)/shard_map/ppermute | solution.py:129
  228.2 13.3 %collective-permute-done.8 = bf16[1024,256]{1,0:T(8,128)(2,1)S(1)} collective-permute-done((bf16[1024,256]{1,0:T(8,128)(2,1)S(1)}, bf16[1024,256]{1,0:T(8,128)(2,1)S(1)}, u32[]{:S(2)}, u32[]{:S(2)}) %collective-permute-start.8) | collective-permute-done | bytes 524320 | tf_op jit(solution)/shard_map/ppermute | solution.py:129
  254.6 6.4 collective-permute-done.12
  261.1 6.4 collective-permute-done.14
  281.3 6.2 collective-permute-done.16
  287.5 6.0 collective-permute-done.18
  306.9 5.8 collective-permute-done.20
  312.7 5.6 collective-permute-done.22
  323.0 10.9 %collective-permute-done.7 = bf16[1024,256]{1,0:T(8,128)(2,1)S(1)} collective-permute-done((bf16[1024,256]{1,0:T(8,128)(2,1)S(1)}, bf16[1024,256]{1,0:T(8,128)(2,1)S(1)}, u32[]{:S(2)}, u32[]{:S(2)}) %collective-permute-start.7) | collective-permute-done | bytes 524320 | tf_op jit(solution)/shard_map/ppermute | solution.py:130
  336.4 11.2 %collective-permute-done.11 = bf16[1024,256]{1,0:T(8,128)(2,1)S(1)} collective-permute-done((bf16[1024,256]{1,0:T(8,128)(2,1)S(1)}, bf16[1024,256]{1,0:T(8,128)(2,1)S(1)}, u32[]{:S(2)}, u32[]{:S(2)}) %collective-permute-start.11) | collective-permute-done | bytes 524320 | tf_op jit(solution)/shard_map/ppermute | solution.py:130
  350.8 12.7 %collective-permute-done.15 = bf16[1024,256]{1,0:T(8,128)(2,1)S(1)} collective-permute-done((bf16[1024,256]{1,0:T(8,128)(2,1)S(1)}, bf16[1024,256]{1,0:T(8,128)(2,1)S(1)}, u32[]{:S(2)}, u32[]{:S(2)}) %collective-permute-start.15) | collective-permute-done | bytes 524320 | tf_op jit(solution)/shard_map/ppermute | solution.py:130
  366.8 14.3 %collective-permute-done.19 = bf16[1024,256]{1,0:T(8,128)(2,1)S(1)} collective-permute-done((bf16[1024,256]{1,0:T(8,128)(2,1)S(1)}, bf16[1024,256]{1,0:T(8,128)(2,1)S(1)}, u32[]{:S(2)}, u32[]{:S(2)}) %collective-permute-start.19) | collective-permute-done | bytes 524320 | tf_op jit(solution)/shard_map/ppermute | solution.py:130
  390.2 5.6 collective-permute-start.26
  401.7 5.9 fusion.179
  413.9 6.1 collective-permute-start.30
  421.4 12.9 %all-reduce.5.cloned.1.call-start = ((), (), s32[]{:S(2)}) async-start(), calls=%async_computation.4 | async-start | bytes 1048576 | tf_op jit(solution)/shard_map/psum | solution.py:172
  440.1 6.2 collective-permute-start.28
  477.7 5.4 fusion.181
  483.1 7.0 fusion.394
  490.1 7.2 convolution_add_fusion.11
  497.3 7.2 convolution_add_fusion.10
  504.6 7.7 convolution_add_fusion.9
  512.2 7.2 convolution_add_fusion.8
  519.5 7.2 convolution_add_fusion.7
  526.7 7.2 fusion.222
  534.0 6.1 fusion.182
  557.2 6.5 collective-permute-done.38
  569.3 5.7 collective-permute-start.40
  591.6 6.5 collective-permute-done.42
  622.0 5.8 collective-permute-done.46
  644.3 7.6 collective-permute-done.49
  655.5 7.6 collective-permute-done.51
  675.0 5.4 collective-permute-start.54
  689.7 15.3 %dynamic_update_slice.14 = f32[4,1024,192]{1,0,2:T(4,128)} dynamic-update-slice(f32[4,1024,192]{1,0,2:T(4,128)} %broadcast_in_dim.32, f32[1,1024,192]{1,0,2:T(1,128)} %copy.41, s32[]{:T(128)S(6)} %select_n.828, s32[]{:T(128)} %constant.77.clone.1, s32[]{:T(128)} %constant.77.clone.1) | dynamic-update-slice | bytes 1572868 | tf_op jit(solution)/shard_map/jit(dynamic_update_index_in_dim)/dynamic_update_slice | solution.py:155
  707.3 5.4 select_select_fusion.1
  722.3 6.8 fusion.404
  729.1 7.1 convolution_add_fusion.5
  736.1 7.1 convolution_add_fusion.4
  743.2 7.1 convolution_add_fusion.3
  750.2 7.2 convolution_add_fusion.2
  757.5 7.1 convolution_add_fusion.1
  764.5 7.1 fusion.221
  774.4 7.5 fusion.414
  781.9 7.5 convolution_add_fusion.17
  789.5 7.5 convolution_add_fusion.16
  797.0 7.5 convolution_add_fusion.15
  804.5 7.9 convolution_add_fusion.14
  812.4 7.5 convolution_add_fusion.13
  820.0 7.5 fusion.223
  829.5 15.2 %dynamic_update_slice.15 = f32[4,1024,192]{1,0,2:T(4,128)} dynamic-update-slice(f32[4,1024,192]{1,0,2:T(4,128)} %dynamic_update_slice.14, f32[1,1024,192]{1,0,2:T(1,128)S(1)} %copy.43, s32[]{:T(128)S(6)} %select_n.878, s32[]{:T(128)} %constant.77.clone.1, s32[]{:T(128)} %constant.77.clone.1) | dynamic-update-slice | bytes 1572868 | tf_op jit(solution)/shard_map/jit(dynamic_update_index_in_dim)/dynamic_update_slice | solution.py:155
  844.7 15.2 %dynamic_update_slice.16 = f32[4,1024,192]{1,0,2:T(4,128)} dynamic-update-slice(f32[4,1024,192]{1,0,2:T(4,128)} %dynamic_update_slice.15, f32[1,1024,192]{1,0,2:T(1,128)S(1)} %copy.45, s32[]{:T(128)S(6)} %select_n.958, s32[]{:T(128)} %constant.77.clone.1, s32[]{:T(128)} %constant.77.clone.1) | dynamic-update-slice | bytes 1572868 | tf_op jit(solution)/shard_map/jit(dynamic_update_index_in_dim)/dynamic_update_slice | solution.py:155
  859.9 15.2 %dynamic_update_slice.17 = f32[4,1024,192]{1,0,2:T(4,128)} dynamic-update-slice(f32[4,1024,192]{1,0,2:T(4,128)} %dynamic_update_slice.16, f32[1,1024,192]{1,0,2:T(1,128)S(1)} %copy-done.70, s32[]{:T(128)S(6)} %select_n.990, s32[]{:T(128)} %constant.77.clone.1, s32[]{:T(128)} %constant.77.clone.1) | dynamic-update-slice | bytes 1572868 | tf_op jit(solution)/shard_map/jit(dynamic_update_index_in_dim)/dynamic_update_slice | solution.py:155
  875.2 5.5 reshape.48
  891.7 124.4 %all-reduce.5.cloned.1.call-done = f32[16,64,128]{2,1,0:T(8,128)} async-done(((f32[16,64,128]{2,1,0:T(8,128)}), f32[16,64,128]{2,1,0:T(8,128)}) %all-reduce.5.cloned.1.call-update) | async-done | bytes 524304 | tf_op jit(solution)/shard_map/psum | solution.py:172
  (438 shorter events, 298.6 us)
Async XLA Ops:
  43.1 53.2 %all-to-all-start.1 = ((bf16[128,4,2048]{0,2,1:T(8,128)(2,1)}), bf16[128,4,2048]{0,2,1:T(8,128)(2,1)}, u32[]{:S(2)}, u32[]{:S(2)}) async-start(bf16[128,4,2048]{0,2,1:T(8,128)(2,1)} %bitcast.238), calls=%async_computation.1 | async-start | bytes 4194304 | tf_op jit(solution)/shard_map/all_to_all | solution.py:45
  48.6 59.2 %all-reduce.3.cloned.1.call-start = ((), (), s32[]{:S(2)}) async-start(), calls=%async_computation.2 | async-start | bytes 1572864 | tf_op jit(solution)/shard_map/psum | solution.py:64
  50.7 350.9 %all-gather.12.cloned.1.call-start = ((), (), s32[]{:S(2)}) async-start(), calls=%async_computation.5 | async-start | bytes 4718592 | tf_op jit(solution)/shard_map/all_gather | solution.py:50
  99.2 335.1 %all-gather.10.cloned.1.call-start = ((), (), s32[]{:S(2)}) async-start(), calls=%async_computation.3 | async-start | bytes 3932160 | tf_op jit(solution)/shard_map/all_gather | solution.py:71
  111.1 372.0 %all-gather.16.cloned.1.call-start = ((), (), s32[]{:S(2)}) async-start(), calls=%async_computation.7 | async-start | bytes 4718592 | tf_op jit(solution)/shard_map/all_gather | solution.py:50
  111.7 610.5 %all-gather.18.cloned.1.call-start = ((), (), s32[]{:S(2)}) async-start(), calls=%async_computation.8 | async-start | bytes 4718592 | tf_op jit(solution)/shard_map/all_gather | solution.py:50
  114.5 16.5 %collective-permute-start = (bf16[1024,256]{1,0:T(8,128)(2,1)}, bf16[1024,256]{1,0:T(8,128)(2,1)S(1)}, u32[]{:S(2)}, u32[]{:S(2)}) collective-permute-start(bf16[1024,256]{1,0:T(8,128)(2,1)} %get-tuple-element.21), channel_id=1, source_target_pairs={{0,1},{1,2},{4,5},{5,6},{8,9},{9,10},{12,13},{13,14},{16,17},{17,1... | collective-permute-start | bytes 1572872 | tf_op jit(solution)/shard_map/ppermute | solution.py:129
  118.4 12.7 %collective-permute-start.1 = (bf16[1024,256]{1,0:T(8,128)(2,1)}, bf16[1024,256]{1,0:T(8,128)(2,1)S(1)}, u32[]{:S(2)}, u32[]{:S(2)}) collective-permute-start(bf16[1024,256]{1,0:T(8,128)(2,1)} %get-tuple-element.21), channel_id=1, source_target_pairs={{3,2},{2,1},{7,6},{6,5},{11,10},{10,9},{15,14},{14,13},{19,18},{18... | collective-permute-start | bytes 1572872 | tf_op jit(solution)/shard_map/ppermute | solution.py:130
  119.1 21.0 %collective-permute-start.2 = (bf16[1024,256]{1,0:T(8,128)(2,1)S(1)}, bf16[1024,256]{1,0:T(8,128)(2,1)S(1)}, u32[]{:S(2)}, u32[]{:S(2)}) collective-permute-start(bf16[1024,256]{1,0:T(8,128)(2,1)S(1)} %get-tuple-element.22), channel_id=1, source_target_pairs={{0,1},{1,2},{4,5},{5,6},{8,9},{9,10},{12,13},{13,14},{16,17},{17,1... | collective-permute-start | bytes 1572872 | tf_op jit(solution)/shard_map/ppermute | solution.py:129
  143.1 20.5 %collective-permute-start.4 = (bf16[1024,256]{1,0:T(8,128)(2,1)}, bf16[1024,256]{1,0:T(8,128)(2,1)S(1)}, u32[]{:S(2)}, u32[]{:S(2)}) collective-permute-start(bf16[1024,256]{1,0:T(8,128)(2,1)} %get-tuple-element.20), channel_id=1, source_target_pairs={{0,1},{1,2},{2,3},{4,5},{5,6},{6,7},{8,9},{9,10},{10,11},{12,13},{... | collective-permute-start | bytes 1572872 | tf_op jit(solution)/shard_map/ppermute | solution.py:129
  147.5 24.4 %collective-permute-start.5 = (bf16[1024,256]{1,0:T(8,128)(2,1)}, bf16[1024,256]{1,0:T(8,128)(2,1)S(1)}, u32[]{:S(2)}, u32[]{:S(2)}) collective-permute-start(bf16[1024,256]{1,0:T(8,128)(2,1)} %get-tuple-element.18), channel_id=1, source_target_pairs={{3,2},{2,1},{1,0},{7,6},{6,5},{5,4},{11,10},{10,9},{9,8},{15,14},{... | collective-permute-start | bytes 1572872 | tf_op jit(solution)/shard_map/ppermute | solution.py:130
  148.8 34.4 %collective-permute-start.6 = (bf16[1024,256]{1,0:T(8,128)(2,1)}, bf16[1024,256]{1,0:T(8,128)(2,1)S(1)}, u32[]{:S(2)}, u32[]{:S(2)}) collective-permute-start(bf16[1024,256]{1,0:T(8,128)(2,1)} %get-tuple-element.19), channel_id=1, source_target_pairs={{0,1},{1,2},{2,3},{4,5},{5,6},{6,7},{8,9},{9,10},{10,11},{12,13},{... | collective-permute-start | bytes 1572872 | tf_op jit(solution)/shard_map/ppermute | solution.py:129
  186.0 42.3 %collective-permute-start.10 = (bf16[1024,256]{1,0:T(8,128)(2,1)S(1)}, bf16[1024,256]{1,0:T(8,128)(2,1)S(1)}, u32[]{:S(2)}, u32[]{:S(2)}) collective-permute-start(bf16[1024,256]{1,0:T(8,128)(2,1)S(1)} %get-tuple-element.16), channel_id=1, source_target_pairs={{0,1},{1,2},{2,3},{4,5},{5,6},{6,7},{8,9},{9,10},{10,11},{12,13},{... | collective-permute-start | bytes 1572872 | tf_op jit(solution)/shard_map/ppermute | solution.py:129
  205.5 36.0 %collective-permute-start.8 = (bf16[1024,256]{1,0:T(8,128)(2,1)S(1)}, bf16[1024,256]{1,0:T(8,128)(2,1)S(1)}, u32[]{:S(2)}, u32[]{:S(2)}) collective-permute-start(bf16[1024,256]{1,0:T(8,128)(2,1)S(1)} %get-tuple-element.17), channel_id=1, source_target_pairs={{0,1},{1,2},{2,3},{4,5},{5,6},{6,7},{8,9},{9,10},{10,11},{12,13},{... | collective-permute-start | bytes 1572872 | tf_op jit(solution)/shard_map/ppermute | solution.py:129
  210.8 30.6 %collective-permute-start.9 = (bf16[1024,256]{1,0:T(8,128)(2,1)S(1)}, bf16[1024,256]{1,0:T(8,128)(2,1)S(1)}, u32[]{:S(2)}, u32[]{:S(2)}) collective-permute-start(bf16[1024,256]{1,0:T(8,128)(2,1)S(1)} %get-tuple-element.15), channel_id=1, source_target_pairs={{3,2},{2,1},{1,0},{7,6},{6,5},{5,4},{11,10},{10,9},{9,8},{15,14},{... | collective-permute-start | bytes 1572872 | tf_op jit(solution)/shard_map/ppermute | solution.py:130
  244.3 16.7 %collective-permute-start.12 = (bf16[1024,256]{1,0:T(8,128)(2,1)S(1)}, bf16[1024,256]{1,0:T(8,128)(2,1)S(1)}, u32[]{:S(2)}, u32[]{:S(2)}) collective-permute-start(bf16[1024,256]{1,0:T(8,128)(2,1)S(1)} %get-tuple-element.14), channel_id=1, source_target_pairs={{0,1},{1,2},{2,3},{4,5},{5,6},{6,7},{8,9},{9,10},{10,11},{12,13},{... | collective-permute-start | bytes 1572872 | tf_op jit(solution)/shard_map/ppermute | solution.py:129
  248.8 12.3 %collective-permute-start.13 = (bf16[1024,256]{1,0:T(8,128)(2,1)S(1)}, bf16[1024,256]{1,0:T(8,128)(2,1)S(1)}, u32[]{:S(2)}, u32[]{:S(2)}) collective-permute-start(bf16[1024,256]{1,0:T(8,128)(2,1)S(1)} %get-tuple-element.12), channel_id=1, source_target_pairs={{3,2},{2,1},{1,0},{7,6},{6,5},{5,4},{11,10},{10,9},{9,8},{15,14},{... | collective-permute-start | bytes 1572872 | tf_op jit(solution)/shard_map/ppermute | solution.py:130
  250.1 17.4 %collective-permute-start.14 = (bf16[1024,256]{1,0:T(8,128)(2,1)S(1)}, bf16[1024,256]{1,0:T(8,128)(2,1)S(1)}, u32[]{:S(2)}, u32[]{:S(2)}) collective-permute-start(bf16[1024,256]{1,0:T(8,128)(2,1)S(1)} %get-tuple-element.13), channel_id=1, source_target_pairs={{0,1},{1,2},{2,3},{4,5},{5,6},{6,7},{8,9},{9,10},{10,11},{12,13},{... | collective-permute-start | bytes 1572872 | tf_op jit(solution)/shard_map/ppermute | solution.py:129
  270.5 17.0 %collective-permute-start.16 = (bf16[1024,256]{1,0:T(8,128)(2,1)}, bf16[1024,256]{1,0:T(8,128)(2,1)S(1)}, u32[]{:S(2)}, u32[]{:S(2)}) collective-permute-start(bf16[1024,256]{1,0:T(8,128)(2,1)} %get-tuple-element.11), channel_id=1, source_target_pairs={{0,1},{1,2},{2,3},{4,5},{5,6},{6,7},{8,9},{9,10},{10,11},{12,13},{... | collective-permute-start | bytes 1572872 | tf_op jit(solution)/shard_map/ppermute | solution.py:129
  274.9 12.6 %collective-permute-start.17 = (bf16[1024,256]{1,0:T(8,128)(2,1)}, bf16[1024,256]{1,0:T(8,128)(2,1)S(1)}, u32[]{:S(2)}, u32[]{:S(2)}) collective-permute-start(bf16[1024,256]{1,0:T(8,128)(2,1)} %get-tuple-element.9), channel_id=1, source_target_pairs={{3,2},{2,1},{1,0},{7,6},{6,5},{5,4},{11,10},{10,9},{9,8},{15,14},{... | collective-permute-start | bytes 1572872 | tf_op jit(solution)/shard_map/ppermute | solution.py:130
  276.2 17.3 %collective-permute-start.18 = (bf16[1024,256]{1,0:T(8,128)(2,1)}, bf16[1024,256]{1,0:T(8,128)(2,1)S(1)}, u32[]{:S(2)}, u32[]{:S(2)}) collective-permute-start(bf16[1024,256]{1,0:T(8,128)(2,1)} %get-tuple-element.10), channel_id=1, source_target_pairs={{0,1},{1,2},{2,3},{4,5},{5,6},{6,7},{8,9},{9,10},{10,11},{12,13},{... | collective-permute-start | bytes 1572872 | tf_op jit(solution)/shard_map/ppermute | solution.py:129
  281.3 493.2 %all-gather.14.cloned.1.call-start = ((), (), s32[]{:S(2)}) async-start(), calls=%async_computation.6 | async-start | bytes 4718592 | tf_op jit(solution)/shard_map/all_gather | solution.py:50
  296.3 16.4 %collective-permute-start.20 = (bf16[1024,256]{1,0:T(8,128)(2,1)S(1)}, bf16[1024,256]{1,0:T(8,128)(2,1)S(1)}, u32[]{:S(2)}, u32[]{:S(2)}) collective-permute-start(bf16[1024,256]{1,0:T(8,128)(2,1)S(1)} %get-tuple-element.8), channel_id=1, source_target_pairs={{0,1},{1,2},{2,3},{4,5},{5,6},{6,7},{8,9},{9,10},{10,11},{12,13},{... | collective-permute-start | bytes 1572872 | tf_op jit(solution)/shard_map/ppermute | solution.py:129
  302.0 16.3 %collective-permute-start.22 = (bf16[1024,256]{1,0:T(8,128)(2,1)S(1)}, bf16[1024,256]{1,0:T(8,128)(2,1)S(1)}, u32[]{:S(2)}, u32[]{:S(2)}) collective-permute-start(bf16[1024,256]{1,0:T(8,128)(2,1)S(1)} %get-tuple-element.7), channel_id=1, source_target_pairs={{0,1},{1,2},{2,3},{4,5},{5,6},{6,7},{8,9},{9,10},{10,11},{12,13},{... | collective-permute-start | bytes 1572872 | tf_op jit(solution)/shard_map/ppermute | solution.py:129
  321.7 12.2 %collective-permute-start.7 = (bf16[1024,256]{1,0:T(8,128)(2,1)S(1)}, bf16[1024,256]{1,0:T(8,128)(2,1)S(1)}, u32[]{:S(2)}, u32[]{:S(2)}) collective-permute-start(bf16[1024,256]{1,0:T(8,128)(2,1)S(1)} %get-tuple-element.5), channel_id=1, source_target_pairs={{3,2},{2,1},{1,0},{7,6},{6,5},{5,4},{11,10},{10,9},{9,8},{15,14},{... | collective-permute-start | bytes 1572872 | tf_op jit(solution)/shard_map/ppermute | solution.py:130
  335.1 12.5 %collective-permute-start.11 = (bf16[1024,256]{1,0:T(8,128)(2,1)S(1)}, bf16[1024,256]{1,0:T(8,128)(2,1)S(1)}, u32[]{:S(2)}, u32[]{:S(2)}) collective-permute-start(bf16[1024,256]{1,0:T(8,128)(2,1)S(1)} %broadcast_select_fusion.32), channel_id=1, source_target_pairs={{3,2},{2,1},{1,0},{7,6},{6,5},{5,4},{11,10},{10,9},{9,8},{15,14},{... | collective-permute-start | bytes 1572872 | tf_op jit(solution)/shard_map/ppermute | solution.py:130
  349.5 14.0 %collective-permute-start.15 = (bf16[1024,256]{1,0:T(8,128)(2,1)S(1)}, bf16[1024,256]{1,0:T(8,128)(2,1)S(1)}, u32[]{:S(2)}, u32[]{:S(2)}) collective-permute-start(bf16[1024,256]{1,0:T(8,128)(2,1)S(1)} %broadcast_select_fusion.30), channel_id=1, source_target_pairs={{3,2},{2,1},{1,0},{7,6},{6,5},{5,4},{11,10},{10,9},{9,8},{15,14},{... | collective-permute-start | bytes 1572872 | tf_op jit(solution)/shard_map/ppermute | solution.py:130
  365.5 15.6 %collective-permute-start.19 = (bf16[1024,256]{1,0:T(8,128)(2,1)S(1)}, bf16[1024,256]{1,0:T(8,128)(2,1)S(1)}, u32[]{:S(2)}, u32[]{:S(2)}) collective-permute-start(bf16[1024,256]{1,0:T(8,128)(2,1)S(1)} %broadcast_select_fusion.28), channel_id=1, source_target_pairs={{3,2},{2,1},{1,0},{7,6},{6,5},{5,4},{11,10},{10,9},{9,8},{15,14},{... | collective-permute-start | bytes 1572872 | tf_op jit(solution)/shard_map/ppermute | solution.py:130
  382.4 15.8 %collective-permute-start.23 = (bf16[1024,256]{1,0:T(8,128)(2,1)S(1)}, bf16[1024,256]{1,0:T(8,128)(2,1)S(1)}, u32[]{:S(2)}, u32[]{:S(2)}) collective-permute-start(bf16[1024,256]{1,0:T(8,128)(2,1)S(1)} %broadcast_select_fusion.26), channel_id=1, source_target_pairs={{3,2},{2,1},{1,0},{7,6},{6,5},{5,4},{11,10},{10,9},{9,8},{15,14},{... | collective-permute-start | bytes 1572872 | tf_op jit(solution)/shard_map/ppermute | solution.py:130
  383.7 23.9 %collective-permute-start.24 = (bf16[1024,256]{1,0:T(8,128)(2,1)}, bf16[1024,256]{1,0:T(8,128)(2,1)S(1)}, u32[]{:S(2)}, u32[]{:S(2)}) collective-permute-start(bf16[1024,256]{1,0:T(8,128)(2,1)} %get-tuple-element.4), channel_id=1, source_target_pairs={{0,1},{1,2},{2,3},{4,5},{5,6},{6,7},{8,9},{9,10},{10,11},{12,13},{... | collective-permute-start | bytes 1572872 | tf_op jit(solution)/shard_map/ppermute | solution.py:129
  388.9 18.7 %collective-permute-start.25 = (bf16[1024,256]{1,0:T(8,128)(2,1)}, bf16[1024,256]{1,0:T(8,128)(2,1)}, u32[]{:S(2)}, u32[]{:S(2)}) collective-permute-start(bf16[1024,256]{1,0:T(8,128)(2,1)} %get-tuple-element.2), channel_id=1, source_target_pairs={{3,2},{2,1},{1,0},{7,6},{6,5},{5,4},{11,10},{10,9},{9,8},{15,14},{... | collective-permute-start | bytes 1572872 | tf_op jit(solution)/shard_map/ppermute | solution.py:130
  390.2 17.4 %collective-permute-start.26 = (bf16[1024,256]{1,0:T(8,128)(2,1)}, bf16[1024,256]{1,0:T(8,128)(2,1)}, u32[]{:S(2)}, u32[]{:S(2)}) collective-permute-start(bf16[1024,256]{1,0:T(8,128)(2,1)} %get-tuple-element.3), channel_id=1, source_target_pairs={{0,1},{1,2},{2,3},{4,5},{5,6},{6,7},{8,9},{9,10},{10,11},{12,13},{... | collective-permute-start | bytes 1572872 | tf_op jit(solution)/shard_map/ppermute | solution.py:129
  400.3 12.1 %collective-permute-start.27 = (bf16[1024,256]{1,0:T(8,128)(2,1)}, bf16[1024,256]{1,0:T(8,128)(2,1)}, u32[]{:S(2)}, u32[]{:S(2)}) collective-permute-start(bf16[1024,256]{1,0:T(8,128)(2,1)} %broadcast_select_fusion.24), channel_id=1, source_target_pairs={{3,2},{2,1},{1,0},{7,6},{6,5},{5,4},{11,10},{10,9},{9,8},{15,14},{... | collective-permute-start | bytes 1572872 | tf_op jit(solution)/shard_map/ppermute | solution.py:130
  413.9 34.1 %collective-permute-start.30 = (bf16[1024,256]{1,0:T(8,128)(2,1)}, bf16[1024,256]{1,0:T(8,128)(2,1)S(1)}, u32[]{:S(2)}, u32[]{:S(2)}) collective-permute-start(bf16[1024,256]{1,0:T(8,128)(2,1)} %get-tuple-element.109), channel_id=1, source_target_pairs={{0,1},{1,2},{2,3},{4,5},{5,6},{6,7},{8,9},{9,10},{10,11},{12,13},{... | collective-permute-start | bytes 1572872 | tf_op jit(solution)/shard_map/ppermute | solution.py:129
  419.9 28.0 %collective-permute-start.31 = (bf16[1024,256]{1,0:T(8,128)(2,1)}, bf16[1024,256]{1,0:T(8,128)(2,1)}, u32[]{:S(2)}, u32[]{:S(2)}) collective-permute-start(bf16[1024,256]{1,0:T(8,128)(2,1)} %get-tuple-element.111), channel_id=1, source_target_pairs={{3,2},{2,1},{1,0},{7,6},{6,5},{5,4},{11,10},{10,9},{9,8},{15,14},{... | collective-permute-start | bytes 1572872 | tf_op jit(solution)/shard_map/ppermute | solution.py:130
  421.4 594.7 %all-reduce.5.cloned.1.call-start = ((), (), s32[]{:S(2)}) async-start(), calls=%async_computation.4 | async-start | bytes 1048576 | tf_op jit(solution)/shard_map/psum | solution.py:172
  440.1 18.7 %collective-permute-start.28 = (bf16[1024,256]{1,0:T(8,128)(2,1)S(1)}, bf16[1024,256]{1,0:T(8,128)(2,1)S(1)}, u32[]{:S(2)}, u32[]{:S(2)}) collective-permute-start(bf16[1024,256]{1,0:T(8,128)(2,1)S(1)} %copy-done.123), channel_id=1, source_target_pairs={{0,1},{1,2},{2,3},{4,5},{5,6},{6,7},{8,9},{9,10},{10,11},{12,13},{... | collective-permute-start | bytes 1572872 | tf_op jit(solution)/shard_map/ppermute | solution.py:129
  446.4 16.1 %collective-permute-start.29 = (bf16[1024,256]{1,0:T(8,128)(2,1)S(1)}, bf16[1024,256]{1,0:T(8,128)(2,1)S(1)}, u32[]{:S(2)}, u32[]{:S(2)}) collective-permute-start(bf16[1024,256]{1,0:T(8,128)(2,1)S(1)} %copy-done.122), channel_id=1, source_target_pairs={{3,2},{2,1},{1,0},{7,6},{6,5},{5,4},{11,10},{10,9},{9,8},{15,14},{... | collective-permute-start | bytes 1572872 | tf_op jit(solution)/shard_map/ppermute | solution.py:130
  457.3 82.8 %collective-permute-start.35 = (bf16[1024,256]{1,0:T(8,128)(2,1)}, bf16[1024,256]{1,0:T(8,128)(2,1)}, u32[]{:S(2)}, u32[]{:S(2)}) collective-permute-start(bf16[1024,256]{1,0:T(8,128)(2,1)} %select_select_fusion.24), channel_id=1, source_target_pairs={{3,2},{2,1},{1,0},{7,6},{6,5},{5,4},{11,10},{10,9},{9,8},{15,14},{... | collective-permute-start | bytes 1572872 | tf_op jit(solution)/shard_map/ppermute | solution.py:130
  465.8 74.3 %collective-permute-start.32 = (bf16[1024,256]{1,0:T(8,128)(2,1)}, bf16[1024,256]{1,0:T(8,128)(2,1)}, u32[]{:S(2)}, u32[]{:S(2)}) collective-permute-start(bf16[1024,256]{1,0:T(8,128)(2,1)} %get-tuple-element.104), channel_id=1, source_target_pairs={{0,1},{1,2},{2,3},{4,5},{5,6},{6,7},{8,9},{9,10},{10,11},{12,13},{... | collective-permute-start | bytes 1572872 | tf_op jit(solution)/shard_map/ppermute | solution.py:129
  471.0 69.1 %collective-permute-start.33 = (bf16[1024,256]{1,0:T(8,128)(2,1)}, bf16[1024,256]{1,0:T(8,128)(2,1)}, u32[]{:S(2)}, u32[]{:S(2)}) collective-permute-start(bf16[1024,256]{1,0:T(8,128)(2,1)} %get-tuple-element.102), channel_id=1, source_target_pairs={{3,2},{2,1},{1,0},{7,6},{6,5},{5,4},{11,10},{10,9},{9,8},{15,14},{... | collective-permute-start | bytes 1572872 | tf_op jit(solution)/shard_map/ppermute | solution.py:130
  472.3 67.8 %collective-permute-start.34 = (bf16[1024,256]{1,0:T(8,128)(2,1)}, bf16[1024,256]{1,0:T(8,128)(2,1)}, u32[]{:S(2)}, u32[]{:S(2)}) collective-permute-start(bf16[1024,256]{1,0:T(8,128)(2,1)} %get-tuple-element.103), channel_id=1, source_target_pairs={{0,1},{1,2},{2,3},{4,5},{5,6},{6,7},{8,9},{9,10},{10,11},{12,13},{... | collective-permute-start | bytes 1572872 | tf_op jit(solution)/shard_map/ppermute | solution.py:129
  540.5 14.4 %collective-permute-start.36 = (bf16[1024,256]{1,0:T(8,128)(2,1)S(1)}, bf16[1024,256]{1,0:T(8,128)(2,1)S(1)}, u32[]{:S(2)}, u32[]{:S(2)}) collective-permute-start(bf16[1024,256]{1,0:T(8,128)(2,1)S(1)} %get-tuple-element.100), channel_id=1, source_target_pairs={{0,1},{1,2},{2,3},{4,5},{5,6},{6,7},{8,9},{9,10},{10,11},{12,13},{... | collective-permute-start | bytes 1572872 | tf_op jit(solution)/shard_map/ppermute | solution.py:129
  543.1 14.1 %collective-permute-start.37 = (bf16[1024,256]{1,0:T(8,128)(2,1)S(1)}, bf16[1024,256]{1,0:T(8,128)(2,1)S(1)}, u32[]{:S(2)}, u32[]{:S(2)}) collective-permute-start(bf16[1024,256]{1,0:T(8,128)(2,1)S(1)} %get-tuple-element.98), channel_id=1, source_target_pairs={{3,2},{2,1},{1,0},{7,6},{6,5},{5,4},{11,10},{10,9},{9,8},{15,14},{... | collective-permute-start | bytes 1572872 | tf_op jit(solution)/shard_map/ppermute | solution.py:130
  544.4 19.3 %collective-permute-start.38 = (bf16[1024,256]{1,0:T(8,128)(2,1)S(1)}, bf16[1024,256]{1,0:T(8,128)(2,1)S(1)}, u32[]{:S(2)}, u32[]{:S(2)}) collective-permute-start(bf16[1024,256]{1,0:T(8,128)(2,1)S(1)} %get-tuple-element.99), channel_id=1, source_target_pairs={{0,1},{1,2},{2,3},{4,5},{5,6},{6,7},{8,9},{9,10},{10,11},{12,13},{... | collective-permute-start | bytes 1572872 | tf_op jit(solution)/shard_map/ppermute | solution.py:129
  549.0 19.5 %collective-permute-start.39 = (bf16[1024,256]{1,0:T(8,128)(2,1)S(1)}, bf16[1024,256]{1,0:T(8,128)(2,1)S(1)}, u32[]{:S(2)}, u32[]{:S(2)}) collective-permute-start(bf16[1024,256]{1,0:T(8,128)(2,1)S(1)} %get-tuple-element.101), channel_id=1, source_target_pairs={{3,2},{2,1},{1,0},{7,6},{6,5},{5,4},{11,10},{10,9},{9,8},{15,14},{... | collective-permute-start | bytes 1572872 | tf_op jit(solution)/shard_map/ppermute | solution.py:130
  569.3 17.8 %collective-permute-start.40 = (bf16[1024,256]{1,0:T(8,128)(2,1)S(1)}, bf16[1024,256]{1,0:T(8,128)(2,1)S(1)}, u32[]{:S(2)}, u32[]{:S(2)}) collective-permute-start(bf16[1024,256]{1,0:T(8,128)(2,1)S(1)} %get-tuple-element.96), channel_id=1, source_target_pairs={{0,1},{1,2},{2,3},{4,5},{5,6},{6,7},{8,9},{9,10},{10,11},{12,13},{... | collective-permute-start | bytes 1572872 | tf_op jit(solution)/shard_map/ppermute | solution.py:129
  575.0 16.6 %collective-permute-start.41 = (bf16[1024,256]{1,0:T(8,128)(2,1)S(1)}, bf16[1024,256]{1,0:T(8,128)(2,1)S(1)}, u32[]{:S(2)}, u32[]{:S(2)}) collective-permute-start(bf16[1024,256]{1,0:T(8,128)(2,1)S(1)} %get-tuple-element.94), channel_id=1, source_target_pairs={{3,2},{2,1},{1,0},{7,6},{6,5},{5,4},{11,10},{10,9},{9,8},{15,14},{... | collective-permute-start | bytes 1572872 | tf_op jit(solution)/shard_map/ppermute | solution.py:130
  576.3 21.8 %collective-permute-start.42 = (bf16[1024,256]{1,0:T(8,128)(2,1)S(1)}, bf16[1024,256]{1,0:T(8,128)(2,1)S(1)}, u32[]{:S(2)}, u32[]{:S(2)}) collective-permute-start(bf16[1024,256]{1,0:T(8,128)(2,1)S(1)} %get-tuple-element.95), channel_id=1, source_target_pairs={{0,1},{1,2},{2,3},{4,5},{5,6},{6,7},{8,9},{9,10},{10,11},{12,13},{... | collective-permute-start | bytes 1572872 | tf_op jit(solution)/shard_map/ppermute | solution.py:129
  580.9 21.4 %collective-permute-start.43 = (bf16[1024,256]{1,0:T(8,128)(2,1)S(1)}, bf16[1024,256]{1,0:T(8,128)(2,1)S(1)}, u32[]{:S(2)}, u32[]{:S(2)}) collective-permute-start(bf16[1024,256]{1,0:T(8,128)(2,1)S(1)} %get-tuple-element.97), channel_id=1, source_target_pairs={{3,2},{2,1},{1,0},{7,6},{6,5},{5,4},{11,10},{10,9},{9,8},{15,14},{... | collective-permute-start | bytes 1572872 | tf_op jit(solution)/shard_map/ppermute | solution.py:130
  603.1 14.5 %collective-permute-start.44 = (bf16[1024,256]{1,0:T(8,128)(2,1)S(1)}, bf16[1024,256]{1,0:T(8,128)(2,1)S(1)}, u32[]{:S(2)}, u32[]{:S(2)}) collective-permute-start(bf16[1024,256]{1,0:T(8,128)(2,1)S(1)} %get-tuple-element.92), channel_id=1, source_target_pairs={{0,1},{1,2},{2,3},{4,5},{5,6},{6,7},{8,9},{9,10},{10,11},{12,13},{... | collective-permute-start | bytes 1572872 | tf_op jit(solution)/shard_map/ppermute | solution.py:129
  605.3 16.7 %collective-permute-start.45 = (bf16[1024,256]{1,0:T(8,128)(2,1)S(1)}, bf16[1024,256]{1,0:T(8,128)(2,1)S(1)}, u32[]{:S(2)}, u32[]{:S(2)}) collective-permute-start(bf16[1024,256]{1,0:T(8,128)(2,1)S(1)} %get-tuple-element.90), channel_id=1, source_target_pairs={{3,2},{2,1},{1,0},{7,6},{6,5},{5,4},{11,10},{10,9},{9,8},{15,14},{... | collective-permute-start | bytes 1572872 | tf_op jit(solution)/shard_map/ppermute | solution.py:130
  606.6 21.2 %collective-permute-start.46 = (bf16[1024,256]{1,0:T(8,128)(2,1)S(1)}, bf16[1024,256]{1,0:T(8,128)(2,1)S(1)}, u32[]{:S(2)}, u32[]{:S(2)}) collective-permute-start(bf16[1024,256]{1,0:T(8,128)(2,1)S(1)} %get-tuple-element.91), channel_id=1, source_target_pairs={{0,1},{1,2},{2,3},{4,5},{5,6},{6,7},{8,9},{9,10},{10,11},{12,13},{... | collective-permute-start | bytes 1572872 | tf_op jit(solution)/shard_map/ppermute | solution.py:129
  611.2 20.8 %collective-permute-start.47 = (bf16[1024,256]{1,0:T(8,128)(2,1)S(1)}, bf16[1024,256]{1,0:T(8,128)(2,1)S(1)}, u32[]{:S(2)}, u32[]{:S(2)}) collective-permute-start(bf16[1024,256]{1,0:T(8,128)(2,1)S(1)} %get-tuple-element.93), channel_id=1, source_target_pairs={{3,2},{2,1},{1,0},{7,6},{6,5},{5,4},{11,10},{10,9},{9,8},{15,14},{... | collective-permute-start | bytes 1572872 | tf_op jit(solution)/shard_map/ppermute | solution.py:130
  635.1 16.8 %collective-permute-start.49 = (bf16[1024,256]{1,0:T(8,128)(2,1)S(1)}, bf16[1024,256]{1,0:T(8,128)(2,1)S(1)}, u32[]{:S(2)}, u32[]{:S(2)}) collective-permute-start(bf16[1024,256]{1,0:T(8,128)(2,1)S(1)} %get-tuple-element.86), channel_id=1, source_target_pairs={{3,2},{2,1},{1,0},{7,6},{6,5},{5,4},{11,10},{10,9},{9,8},{15,14},{... | collective-permute-start | bytes 1572872 | tf_op jit(solution)/shard_map/ppermute | solution.py:130
  636.4 19.1 %collective-permute-start.50 = (bf16[1024,256]{1,0:T(8,128)(2,1)S(1)}, bf16[1024,256]{1,0:T(8,128)(2,1)S(1)}, u32[]{:S(2)}, u32[]{:S(2)}) collective-permute-start(bf16[1024,256]{1,0:T(8,128)(2,1)S(1)} %get-tuple-element.87), channel_id=1, source_target_pairs={{0,1},{1,2},{2,3},{4,5},{5,6},{6,7},{8,9},{9,10},{10,11},{12,13},{... | collective-permute-start | bytes 1572872 | tf_op jit(solution)/shard_map/ppermute | solution.py:129
  641.0 22.1 %collective-permute-start.51 = (bf16[1024,256]{1,0:T(8,128)(2,1)S(1)}, bf16[1024,256]{1,0:T(8,128)(2,1)S(1)}, u32[]{:S(2)}, u32[]{:S(2)}) collective-permute-start(bf16[1024,256]{1,0:T(8,128)(2,1)S(1)} %get-tuple-element.89), channel_id=1, source_target_pairs={{3,2},{2,1},{1,0},{7,6},{6,5},{5,4},{11,10},{10,9},{9,8},{15,14},{... | collective-permute-start | bytes 1572872 | tf_op jit(solution)/shard_map/ppermute | solution.py:130
  665.9 14.5 %collective-permute-start.53 = (bf16[1024,256]{1,0:T(8,128)(2,1)S(1)}, bf16[1024,256]{1,0:T(8,128)(2,1)}, u32[]{:S(2)}, u32[]{:S(2)}) collective-permute-start(bf16[1024,256]{1,0:T(8,128)(2,1)S(1)} %get-tuple-element.82), channel_id=1, source_target_pairs={{3,2},{2,1},{1,0},{7,6},{6,5},{5,4},{11,10},{10,9},{9,8},{15,14},{... | collective-permute-start | bytes 1572872 | tf_op jit(solution)/shard_map/ppermute | solution.py:130
  667.2 14.5 %collective-permute-start.52 = (bf16[1024,256]{1,0:T(8,128)(2,1)S(1)}, bf16[1024,256]{1,0:T(8,128)(2,1)}, u32[]{:S(2)}, u32[]{:S(2)}) collective-permute-start(bf16[1024,256]{1,0:T(8,128)(2,1)S(1)} %get-tuple-element.84), channel_id=1, source_target_pairs={{0,1},{1,2},{2,3},{4,5},{5,6},{6,7},{8,9},{9,10},{10,11},{12,13},{... | collective-permute-start | bytes 1572872 | tf_op jit(solution)/shard_map/ppermute | solution.py:129
  673.5 31.5 %collective-permute-start.55 = (bf16[1024,256]{1,0:T(8,128)(2,1)}, bf16[1024,256]{1,0:T(8,128)(2,1)}, u32[]{:S(2)}, u32[]{:S(2)}) collective-permute-start(bf16[1024,256]{1,0:T(8,128)(2,1)} %get-tuple-element.85), channel_id=1, source_target_pairs={{3,2},{2,1},{1,0},{7,6},{6,5},{5,4},{11,10},{10,9},{9,8},{15,14},{... | collective-permute-start | bytes 1572872 | tf_op jit(solution)/shard_map/ppermute | solution.py:130
  675.0 31.6 %collective-permute-start.54 = (bf16[1024,256]{1,0:T(8,128)(2,1)}, bf16[1024,256]{1,0:T(8,128)(2,1)}, u32[]{:S(2)}, u32[]{:S(2)}) collective-permute-start(bf16[1024,256]{1,0:T(8,128)(2,1)} %get-tuple-element.83), channel_id=1, source_target_pairs={{0,1},{1,2},{2,3},{4,5},{5,6},{6,7},{8,9},{9,10},{10,11},{12,13},{... | collective-permute-start | bytes 1572872 | tf_op jit(solution)/shard_map/ppermute | solution.py:129
  680.4 26.9 %collective-permute-start.56 = (bf16[1024,256]{1,0:T(8,128)(2,1)}, bf16[1024,256]{1,0:T(8,128)(2,1)}, u32[]{:S(2)}, u32[]{:S(2)}) collective-permute-start(bf16[1024,256]{1,0:T(8,128)(2,1)} %collective-permute-done.53), channel_id=1, source_target_pairs={{1,0},{5,4},{9,8},{13,12},{17,16},{21,20},{25,24},{29,28}} | collective-permute-start | bytes 1572872 | tf_op jit(solution)/shard_map/ppermute | solution.py:130
  681.7 25.7 %collective-permute-start.57 = (bf16[1024,256]{1,0:T(8,128)(2,1)}, bf16[1024,256]{1,0:T(8,128)(2,1)}, u32[]{:S(2)}, u32[]{:S(2)}) collective-permute-start(bf16[1024,256]{1,0:T(8,128)(2,1)} %collective-permute-done.52), channel_id=1, source_target_pairs={{2,3},{6,7},{10,11},{14,15},{18,19},{22,23},{26,27},{30,31}} | collective-permute-start | bytes 1572872 | tf_op jit(solution)/shard_map/ppermute | solution.py:129
  705.0 12.3 %collective-permute-start.58 = (bf16[1024,256]{1,0:T(8,128)(2,1)}, bf16[1024,256]{1,0:T(8,128)(2,1)S(1)}, u32[]{:S(2)}, u32[]{:S(2)}) collective-permute-start(bf16[1024,256]{1,0:T(8,128)(2,1)} %collective-permute-done.55), channel_id=1, source_target_pairs={{1,0},{5,4},{9,8},{13,12},{17,16},{21,20},{25,24},{29,28}} | collective-permute-start | bytes 1572872 | tf_op jit(solution)/shard_map/ppermute | solution.py:130
  (137 other events, 2125.0 us)
Sparse Core Ops, SparseCore 0:
  52.6 55.1 all-reduce.2
  109.7 36.6 all-gather.11
  147.9 91.7 all-gather.9
  241.5 37.2 all-gather.15
  281.4 36.5 all-gather.17
  421.5 39.2 all-gather.13
  891.8 124.2 all-reduce.4

commit v2 on v1

v2 whole, which is shorter than its diff:
```python
import jax
import jax.numpy as jnp
from jax import lax
from jax.sharding import PartitionSpec as P

K1 = 64
K2 = 128
SEQ = 256
CHUNKS = 4


def contract_last(left, right):
    return lax.dot_general(
        left, right, (((1,), (1,)), ((), ())), preferred_element_type=jnp.float32
    )


def body(
    grad_out,
    inputs,
    gate_pre,
    down_weight,
    input_adapter_factor,
    adapter_second,
    sketch_model,
    sketch_hidden,
    mixer_first,
    second_sign_mixer,
):
    z = lax.axis_index("dp")
    planes = lax.axis_size("dp")
    ranks = lax.axis_size("fsdp")
    outer = (z == 0) | (z == 3)
    low = z < 2
    tokens, hidden = gate_pre.shape
    width = hidden // CHUNKS
    span = width
    rank = adapter_second.shape[0]

    own = [gate_pre[:, i * width : (i + 1) * width] for i in range(CHUNKS)]

    inward = [(0, 1), (3, 2)]
    across = [(1, 2), (2, 1)]
    outward = [(1, 0), (2, 3)]
    near = [lax.ppermute(v, "dp", inward) for v in own]
    far_inner = [lax.ppermute(v, "dp", across) for v in own]
    grad_out, near[0], far_inner[0] = lax.optimization_barrier(
        (grad_out, near[0], far_inner[0])
    )
    far_outer = [lax.ppermute(v, "dp", outward) for v in far_inner]
    last_inner = [lax.ppermute(v, "dp", across) for v in near]
    last_outer = [lax.ppermute(v, "dp", outward) for v in last_inner]

    rows = lax.all_to_all(grad_out, "fsdp", 0, 1, tiled=True)
    rows = lax.all_to_all(rows, "dp", 1, 0, tiled=True)
    rows = rows.reshape(planes, tokens // ranks, down_weight.shape[1])

    def gathered(block):
        piece = lax.dynamic_index_in_dim(rows, block, 0, keepdims=False)
        return lax.all_gather(piece, "fsdp", axis=0, tiled=True)

    block_a = z ^ 1
    block_c = jnp.where(low, 2, 1)
    block_d = jnp.where(low, 3, 0)
    grad_a = gathered(block_a)
    grad_c = gathered(block_c)
    grad_b = gathered(z)
    grad_d = gathered(block_d)

    model_factors = jnp.concatenate(
        [input_adapter_factor, sketch_model.astype(jnp.bfloat16)], axis=1
    )
    model_side = jnp.dot(inputs, model_factors, preferred_element_type=jnp.float32)
    model_side = lax.psum(model_side, "fsdp")
    second_right = jnp.dot(
        model_side[:, :rank].astype(jnp.bfloat16),
        second_sign_mixer.astype(jnp.bfloat16),
        preferred_element_type=jnp.float32,
    )
    model_side = jnp.concatenate([second_right, model_side[:, rank:]], axis=1)
    model_side = lax.all_gather(model_side, "dp", axis=0, tiled=True)

    hidden_factors = jnp.concatenate(
        [adapter_second, sketch_hidden.astype(jnp.bfloat16).T], axis=0
    )

    def silu(v):
        return jax.nn.silu(v.astype(jnp.float32))

    def upstream(grad, group):
        return contract_last(grad, down_weight[group * span : (group + 1) * span])

    def sketched(scaled, group):
        return contract_last(scaled, hidden_factors[:, group * span : (group + 1) * span])

    total_a = total_b = total_c = total_d = 0.0
    neighbour = []
    for i in range(CHUNKS):
        up = upstream(grad_a, i)
        scaled = jnp.where(outer, up, up * silu(near[i])).astype(jnp.bfloat16)
        total_a = total_a + sketched(scaled, i)
        neighbour.append(lax.ppermute(scaled, "dp", inward))
    for i in range(CHUNKS):
        gate = jnp.where(outer, far_outer[i], far_inner[i])
        scaled = (upstream(grad_c, i) * silu(gate)).astype(jnp.bfloat16)
        total_c = total_c + sketched(scaled, i)
    for i in range(CHUNKS):
        up = upstream(grad_b, i) + jnp.where(outer, 0.0, neighbour[i].astype(jnp.float32))
        scaled = (up * silu(own[i])).astype(jnp.bfloat16)
        total_b = total_b + sketched(scaled, i)
        gate = jnp.where(outer, last_outer[i], last_inner[i])
        scaled = (upstream(grad_d, i) * silu(gate)).astype(jnp.bfloat16)
        total_d = total_d + sketched(scaled, i)

    total_a = jnp.where(outer, 0.0, total_a)
    low_pair = jnp.stack([jnp.where(z == 0, total_b, total_a), jnp.where(z == 0, total_a, total_b)])
    high_pair = jnp.stack([jnp.where(z == 2, total_b, total_a), jnp.where(z == 2, total_a, total_b)])
    others = jnp.stack([jnp.where(low, total_c, total_d), jnp.where(low, total_d, total_c)])
    sums = jnp.concatenate(
        [jnp.where(low, low_pair, others), jnp.where(low, others, high_pair)], axis=0
    )

    count = tokens // SEQ
    sums = sums.reshape(planes * count, SEQ, rank + K1)
    model_side = model_side.reshape(planes * count, SEQ, K2 + K1)
    back, left_hidden = sums[..., :rank], sums[..., rank:]
    second_right, left_model = model_side[..., :K2], model_side[..., K2:]
    projected = jnp.einsum(
        "esa,esb->eab", left_hidden, second_right, precision=lax.Precision.HIGHEST
    )
    crossed = jnp.einsum("esa,esr->ear", left_model, back, precision=lax.Precision.HIGHEST)
    projected = projected + jnp.einsum(
        "ear,rb->eab",
        crossed,
        mixer_first.astype(jnp.float32),
        precision=lax.Precision.HIGHEST,
    )
    projected = projected.reshape(planes, count, K1 * K2)
    projected = lax.all_to_all(projected, "dp", 0, 0, tiled=True)
    projected = lax.psum(jnp.sum(projected, axis=0), "fsdp")
    features = projected * lax.rsqrt(jnp.mean(projected * projected, axis=1, keepdims=True) + 1e-06)
    centre = jnp.sum(lax.all_gather(jnp.sum(features, axis=0), "dp"), axis=0) / (planes * count)
    scores = jnp.dot(features, centre, precision=lax.Precision.HIGHEST) / (
        K1 * K2 * jnp.sqrt(jnp.mean(centre * centre) + 1e-06)
    )
    return (features, scores)


def solution(mesh):
    placed = (
        P("dp", "fsdp"),
        P("dp", "fsdp"),
        P("dp", "fsdp"),
        P("fsdp", "dp"),
        P("fsdp", None),
        P(None, "fsdp"),
        P("fsdp", None),
        P("fsdp", None),
        P(),
        P(),
    )
    return jax.shard_map(
        body, mesh=mesh, in_specs=placed, out_specs=(P("dp", None), P("dp")), check_vma=False
    )
```

time: 1040 us -> 815 us (0.78)
  starting transfers between devices: 206 us -> 91.1 us
  local copies, waits for them, and re-layouts: 98.7 us -> 27.2 us
  other arithmetic: 52.2 us -> 8.81 us
  waiting for transfers between devices: 418 us -> 449 us
  matrix products: 206 us -> 187 us
    ppermute x60 -> x24, starting transfers between devices: 187 us -> 81.1 us  [the longest x4 36.5 us: body(): neighbour.append(lax.ppermute(scaled, 'dp', inward))]
    psum x1, waiting for transfers between devices: 124 us -> 55.9 us  [body(): projected = lax.psum(jnp.sum(projected, axis=0), 'fsdp')]
    dynamic_update_slice x4 -> x0, local copies, waits for them, and re-layouts: 61 us -> none  [body(): sums = lax.dynamic_update_index_in_dim(sums, total, block, 0)]
    all_to_all x1, waiting for transfers between devices: 45.5 us -> 93.7 us  [body(): rows = lax.all_to_all(rows, 'dp', 1, 0, tiled=True)]
    select_n x22 -> x1, other arithmetic: 48 us -> 2.36 us  [body(): jnp.where(low, low_pair, others)]
    ppermute x60 -> x24, waiting for transfers between devices: 239 us -> 272 us  [the longest x4 122 us: body(): near = [lax.ppermute(v, 'dp', inward) for v in own]]
    dot_general x35 -> x20, matrix products: 192 us -> 174 us  [contract_last(): lax.dot_general(left, right, (((1,), (1,)), ((), ())), preferred_element_...]
    all_to_all x1, blocking collectives: 32 us -> 15.8 us  [body(): projected = lax.all_to_all(projected, 'dp', 0, 0, tiled=True)]
  transfers between devices with their start and end apart: 68 -> 33, of which waited for: 39 -> 13; matrix products, arithmetic and copies ran while one was open for 22% -> 22% of each run, Pallas kernels for 0% -> 0%
where the time goes in v2:
time: 815 us; the launch traced here: 809 us
  waiting for transfers between devices  449 us (55%)
  matrix products  187 us (23%)
  starting transfers between devices  91.1 us (11%)
  blocking collectives  29.2 us (4%)
  local copies, waits for them, and re-layouts  27.2 us (3%)
  between operations  15.8 us (2%)
  other arithmetic  8.81 us (1%)
    dot_general x20, matrix products, contract_last(): lax.dot_general(left, right, (((1,), (1,)), ((), ())), preferred_element_...  174 us
    ppermute x4, waiting for transfers between devices, body(): near = [lax.ppermute(v, 'dp', inward) for v in own]  122 us
    all_to_all x1, waiting for transfers between devices, body(): rows = lax.all_to_all(rows, 'dp', 1, 0, tiled=True)  93.7 us
    ppermute x4, waiting for transfers between devices, body(): last_outer = [lax.ppermute(v, 'dp', outward) for v in last_inner]  92.4 us
    psum x1, waiting for transfers between devices, body(): projected = lax.psum(jnp.sum(projected, axis=0), 'fsdp')  55.9 us
    ppermute x4, waiting for transfers between devices, body(): neighbour.append(lax.ppermute(scaled, 'dp', inward))  41.5 us
    ppermute x4, starting transfers between devices, body(): neighbour.append(lax.ppermute(scaled, 'dp', inward))  36.5 us
    psum x1, waiting for transfers between devices, body(): model_side = lax.psum(model_side, 'fsdp')  21.5 us
  transfers between devices with their start and end apart: 33, of which 13 were waited for; matrix products, arithmetic and copies ran while one was open for 22% of the time, Pallas kernels for 0%

profile of v2, /device:TPU:0, one launch (start us, length us, event | category | flops | bytes accessed | tf_op | source)
XLA Modules:
  0.0 808.7 jit_solution(12993061362119827144)
XLA Ops:
  7.2 6.4 fusion.367
  13.7 6.2 collective-permute-start
  19.8 2.0 collective-permute-start.1
  22.0 1.8 convolution_bitcast_fusion
  23.8 34.4 %collective-permute-done = bf16[1024,896]{1,0:T(8,128)(2,1)} collective-permute-done((bf16[1024,896]{1,0:T(8,128)(2,1)}, bf16[1024,896]{1,0:T(8,128)(2,1)}, u32[]{:S(2)}, u32[]{:S(2)}) %collective-permute-start) | collective-permute-done | bytes 1835040 | tf_op jit(solution)/shard_map/ppermute | solution.py:45
  58.2 3.7 all-to-all-start
  61.9 21.5 %all-reduce.3.cloned.1.call-done = f32[1024,192]{0,1:T(8,128)} async-done(((f32[1024,192]{0,1:T(8,128)}), f32[1024,192]{0,1:T(8,128)}) %all-reduce.3.cloned.1.call-update) | async-done | bytes 786448 | tf_op jit(solution)/shard_map/psum | solution.py:74
  86.7 4.9 all-to-all-done
  91.7 2.4 copy.44
  94.0 6.1 all-to-all-start.1
  100.1 93.7 %all-to-all-done.1 = bf16[128,4,2048]{0,2,1:T(8,128)(2,1)S(1)} async-done(((bf16[128,4,2048]{0,2,1:T(8,128)(2,1)}), bf16[128,4,2048]{0,2,1:T(8,128)(2,1)S(1)}, u32[]{:S(2)}, u32[]{:S(2)}) %all-to-all-start.1) | async-done | bytes 2097184 | tf_op jit(solution)/shard_map/all_to_all | solution.py:55
  196.4 2.5 collective-permute-start.3
  198.9 1.9 collective-permute-start.10
  200.8 1.8 collective-permute-start.16
  202.7 1.9 collective-permute-start.14
  204.6 4.3 collective-permute-start.7
  208.9 29.6 %collective-permute-done.3 = bf16[1024,896]{1,0:T(8,128)(2,1)} collective-permute-done((bf16[1024,896]{1,0:T(8,128)(2,1)}, bf16[1024,896]{1,0:T(8,128)(2,1)}, u32[]{:S(2)}, u32[]{:S(2)}) %collective-permute-start.3) | collective-permute-done | bytes 1835040 | tf_op jit(solution)/shard_map/ppermute | solution.py:45
  238.5 5.6 collective-permute-start.5
  246.8 1.4 pad_maximum_fusion.3
  248.2 3.3 copy.59
  252.6 1.5 slice.106
  254.2 1.9 collective-permute-start.12
  256.1 21.6 %collective-permute-done.7 = bf16[1024,896]{1,0:T(8,128)(2,1)} collective-permute-done((bf16[1024,896]{1,0:T(8,128)(2,1)}, bf16[1024,896]{1,0:T(8,128)(2,1)}, u32[]{:S(2)}, u32[]{:S(2)}) %collective-permute-start.7) | collective-permute-done | bytes 1835040 | tf_op jit(solution)/shard_map/ppermute | solution.py:45
  277.8 1.9 collective-permute-start.18
  279.7 35.9 %collective-permute-done.5 = bf16[1024,896]{1,0:T(8,128)(2,1)} collective-permute-done((bf16[1024,896]{1,0:T(8,128)(2,1)}, bf16[1024,896]{1,0:T(8,128)(2,1)}, u32[]{:S(2)}, u32[]{:S(2)}) %collective-permute-start.5) | collective-permute-done | bytes 1835040 | tf_op jit(solution)/shard_map/ppermute | solution.py:45
  316.9 1.9 collective-permute-start.22
  318.8 5.8 collective-permute-done.17
  324.6 2.1 collective-permute-start.20
  326.8 10.1 %fusion.152 = f32[1024,192]{0,1:T(8,128)} fusion(bf16[192,896]{1,0:T(8,128)(2,1)S(1)} %get-tuple-element.27, bf16[1024,896]{1,0:T(8,128)(2,1)} %collective-permute-done.17, bf16[1024,896]{1,0:T(8,128)(2,1)} %collective-permute-done.16, pred[]{:T(512)S(6)} %or.3, bf16[1024,1,2048]{0,2,1:T(8,128)(2,1)} %all-gather.19.cloned.1.call-done, ...), kind=kOutput, calls=%fused_computation.172 | convolution fusion | flops 4117757952 | bytes 12664833 | tf_op jit(solution)/shard_map/dot_general | solution.py:13
  336.9 10.2 %fusion.144 = f32[1024,192]{0,1:T(8,128)} fusion(bf16[192,896]{1,0:T(8,128)(2,1)S(1)} %get-tuple-element.27, bf16[1024,896]{1,0:T(8,128)(2,1)} %collective-permute-done.9, bf16[1024,896]{1,0:T(8,128)(2,1)} %collective-permute-done.1, pred[]{:T(512)S(6)} %or.3, bf16[1024,1,2048]{0,2,1:T(8,128)(2,1)} %all-gather.17.cloned.1.call-done, ...), kind=kOutput, calls=%fused_computation.168 | convolution fusion | flops 4117757952 | bytes 12664833 | tf_op jit(solution)/shard_map/dot_general | solution.py:13
  349.7 16.8 %collective-permute-done.15 = bf16[1024,896]{1,0:T(8,128)(2,1)} collective-permute-done((bf16[1024,896]{1,0:T(8,128)(2,1)}, bf16[1024,896]{1,0:T(8,128)(2,1)}, u32[]{:S(2)}, u32[]{:S(2)}) %collective-permute-start.15) | collective-permute-done | bytes 1835040 | tf_op jit(solution)/shard_map/ppermute | solution.py:50
  369.1 1.5 collective-permute-start.21
  370.7 10.1 %fusion.150 = f32[1024,192]{0,1:T(8,128)} fusion(bf16[192,896]{1,0:T(8,128)(2,1)S(1)} %get-tuple-element.26, bf16[1024,896]{1,0:T(8,128)(2,1)} %collective-permute-done.15, bf16[1024,896]{1,0:T(8,128)(2,1)} %collective-permute-done.14, pred[]{:T(512)S(6)} %or.3, bf16[1024,1,2048]{0,2,1:T(8,128)(2,1)} %all-gather.17.cloned.1.call-done, ...), kind=kOutput, calls=%fused_computation.171 | convolution fusion | flops 4117757952 | bytes 12664833 | tf_op jit(solution)/shard_map/dot_general | solution.py:13
  380.8 10.2 %fusion.101 = bf16[1024,896]{1,0:T(8,128)(2,1)} fusion(bf16[1024,896]{1,0:T(8,128)(2,1)} %collective-permute-done.3, bf16[3584,2048]{1,0:T(8,128)(2,1)} %param.13, bf16[1024,1,2048]{0,2,1:T(8,128)(2,1)} %all-gather.15.cloned.1.call-done, pred[]{:T(512)S(6)} %or.3), kind=kOutput, calls=%fused_computation.137 | convolution fusion | flops 3765436416 | bytes 11534337 | tf_op jit(solution)/shard_map/dot_general | solution.py:13
  390.9 8.0 fusion.102
  398.9 85.6 %collective-permute-done.19 = bf16[1024,896]{1,0:T(8,128)(2,1)} collective-permute-done((bf16[1024,896]{1,0:T(8,128)(2,1)}, bf16[1024,896]{1,0:T(8,128)(2,1)}, u32[]{:S(2)}, u32[]{:S(2)}) %collective-permute-start.19) | collective-permute-done | bytes 1835040 | tf_op jit(solution)/shard_map/ppermute | solution.py:52
  484.5 27.9 %collective-permute-start.4 = (bf16[1024,896]{1,0:T(8,128)(2,1)}, bf16[1024,896]{1,0:T(8,128)(2,1)}, u32[]{:S(2)}, u32[]{:S(2)}) collective-permute-start(bf16[1024,896]{1,0:T(8,128)(2,1)} %fusion.101), channel_id=1, source_target_pairs={{0,1},{3,2},{4,5},{7,6},{8,9},{11,10},{12,13},{15,14},{16,17},{19,... | collective-permute-start | bytes 5505032 | tf_op jit(solution)/shard_map/ppermute | solution.py:102
  512.4 10.3 %fusion.293 = f32[1024,192]{0,1:T(8,128)} fusion(f32[1024,192]{0,1:T(8,128)} %fusion.152, bf16[192,896]{1,0:T(8,128)(2,1)S(1)} %get-tuple-element.28, bf16[1024,896]{1,0:T(8,128)(2,1)} %collective-permute-done.19, bf16[1024,896]{1,0:T(8,128)(2,1)} %collective-permute-done.18, pred[]{:T(512)S(6)} %or.3, bf16[3584,2048]{1,0:T(8,128)(2,1)} %param.13, ...), kind=kOutput, calls=%fused_computation.195 | convolution fusion | flops 4117954560 | bytes 13451265 | tf_op jit(solution)/shard_map/dot_general | solution.py:13
  523.8 2.9 collective-permute-start.6
  526.7 10.1 %fusion.158 = f32[1024,192]{0,1:T(8,128)} fusion(bf16[192,896]{1,0:T(8,128)(2,1)S(1)} %copy-done.10, bf16[1024,896]{1,0:T(8,128)(2,1)} %collective-permute-done.23, bf16[1024,896]{1,0:T(8,128)(2,1)} %collective-permute-done.22, pred[]{:T(512)S(6)} %or.3, bf16[1024,1,2048]{0,2,1:T(8,128)(2,1)} %all-gather.19.cloned.1.call-done, bf16[3584,2048]{1,0:T(8,128)(2,1)} %param.13), kind=kOutput, calls=%fused_computation.175 | convolution fusion | flops 4117757952 | bytes 12664833 | tf_op jit(solution)/shard_map/dot_general | solution.py:13
  536.8 10.1 %fusion.100 = bf16[1024,896]{1,0:T(8,128)(2,1)} fusion(bf16[1024,896]{1,0:T(8,128)(2,1)} %collective-permute-done, bf16[3584,2048]{1,0:T(8,128)(2,1)} %param.13, bf16[1024,1,2048]{0,2,1:T(8,128)(2,1)} %all-gather.15.cloned.1.call-done, pred[]{:T(512)S(6)} %or.3), kind=kOutput, calls=%fused_computation.136 | convolution fusion | flops 3765436416 | bytes 11534337 | tf_op jit(solution)/shard_map/dot_general | solution.py:13
  546.9 2.7 collective-permute-start.2
  549.6 10.1 %fusion.314 = f32[1024,192]{0,1:T(8,128)} fusion(f32[1024,192]{0,1:T(8,128)S(1)} %copy-done.23, bf16[192,896]{1,0:T(8,128)(2,1)S(1)} %get-tuple-element.28, bf16[1024,896]{1,0:T(8,128)(2,1)} %collective-permute-done.11, bf16[1024,896]{1,0:T(8,128)(2,1)} %collective-permute-done.10, pred[]{:T(512)S(6)} %or.3, bf16[3584,2048]{1,0:T(8,128)(2,1)} %param.13, ...), kind=kOutput, calls=%fused_computation.198 | convolution fusion | flops 4117954560 | bytes 13451265 | tf_op jit(solution)/shard_map/dot_general | solution.py:13
  559.7 10.1 %fusion.103 = bf16[1024,896]{1,0:T(8,128)(2,1)} fusion(bf16[1024,896]{1,0:T(8,128)(2,1)} %collective-permute-done.7, bf16[3584,2048]{1,0:T(8,128)(2,1)} %param.13, bf16[1024,1,2048]{0,2,1:T(8,128)(2,1)} %all-gather.15.cloned.1.call-done, pred[]{:T(512)S(6)} %or.3), kind=kOutput, calls=%fused_computation.139 | convolution fusion | flops 3765436416 | bytes 11534337 | tf_op jit(solution)/shard_map/dot_general | solution.py:13
  569.8 2.3 fusion.380
  572.1 2.3 convolution_add_fusion.2
  574.4 3.0 collective-permute-start.8
  577.4 10.5 %fusion.307 = f32[1024,192]{0,1:T(8,128)} fusion(f32[1024,192]{0,1:T(8,128)} %fusion.150, f32[1024,192]{0,1:T(8,128)} %fusion.314, bf16[192,896]{1,0:T(8,128)(2,1)S(1)} %get-tuple-element.29, bf16[1024,896]{1,0:T(8,128)(2,1)} %collective-permute-done.13, bf16[1024,896]{1,0:T(8,128)(2,1)} %collective-permute-done.12, pred[]{:T(512)S(6)} %or.3, ...), kind=kOutput, calls=%fused_computation.197 | convolution fusion | flops 4118151168 | bytes 14237697 | tf_op jit(solution)/shard_map/dot_general | solution.py:13
  587.9 11.0 %select_bitcast_fusion.3 = (f32[1,1024,192]{1,2,0:T(8,128)}, f32[1,1024,192]{1,2,0:T(8,128)}) fusion(f32[1024,192]{0,1:T(8,128)} %fusion.307, pred[]{:T(512)S(6)} %lt.13, f32[1024,192]{0,1:T(8,128)} %fusion.158, f32[1024,192]{0,1:T(8,128)} %fusion.293, bf16[192,896]{1,0:T(8,128)(2,1)S(1)} %get-tuple-element.29, ...), kind=kOutput, calls=%fused_computation.209 | convolution fusion | flops 4118544384 | bytes 15810562 | tf_op jit(solution)/shard_map/dot_general | solution.py:13
  599.8 3.2 fusion.264
  603.0 11.0 %fusion.162 = f32[1024,192]{0,1:T(8,128)} fusion(bf16[192,896]{1,0:T(8,128)(2,1)S(1)} %get-tuple-element.28, bf16[1024,896]{1,0:T(8,128)(2,1)} %collective-permute-done.4, pred[]{:T(512)S(6)} %or.3, bf16[1024,1,2048]{0,2,1:T(8,128)(2,1)} %all-gather.13.cloned.1.call-done, bf16[3584,2048]{1,0:T(8,128)(2,1)} %param.13, bf16[1024,3584]{1,0:T(8,128)(2,1)} %param.12), kind=kOutput, calls=%fused_computation.177 | convolution fusion | flops 4119592960 | bytes 12664833 | tf_op jit(solution)/shard_map/dot_general | solution.py:13
  613.9 10.8 %fusion.164 = f32[1024,192]{0,1:T(8,128)} fusion(bf16[192,896]{1,0:T(8,128)(2,1)S(1)} %get-tuple-element.29, bf16[1024,896]{1,0:T(8,128)(2,1)} %collective-permute-done.6, pred[]{:T(512)S(6)} %or.3, bf16[1024,1,2048]{0,2,1:T(8,128)(2,1)} %all-gather.13.cloned.1.call-done, bf16[3584,2048]{1,0:T(8,128)(2,1)} %param.13, bf16[1024,3584]{1,0:T(8,128)(2,1)} %param.12), kind=kOutput, calls=%fused_computation.178 | convolution fusion | flops 4119592960 | bytes 12664833 | tf_op jit(solution)/shard_map/dot_general | solution.py:13
  624.7 41.5 %collective-permute-done.8 = bf16[1024,896]{1,0:T(8,128)(2,1)} collective-permute-done((bf16[1024,896]{1,0:T(8,128)(2,1)}, bf16[1024,896]{1,0:T(8,128)(2,1)}, u32[]{:S(2)}, u32[]{:S(2)}) %collective-permute-start.8) | collective-permute-done | bytes 1835040 | tf_op jit(solution)/shard_map/ppermute | solution.py:102
  666.2 11.0 %fusion.166 = f32[1024,192]{0,1:T(8,128)} fusion(bf16[192,896]{1,0:T(8,128)(2,1)S(1)} %copy-done.12, bf16[1024,896]{1,0:T(8,128)(2,1)} %collective-permute-done.8, pred[]{:T(512)S(6)} %or.3, bf16[1024,1,2048]{0,2,1:T(8,128)(2,1)} %all-gather.13.cloned.1.call-done, bf16[3584,2048]{1,0:T(8,128)(2,1)} %param.13, bf16[1024,3584]{1,0:T(8,128)(2,1)} %param.12), kind=kOutput, calls=%fused_computation.179 | convolution fusion | flops 4119592960 | bytes 12664833 | tf_op jit(solution)/shard_map/dot_general | solution.py:13
  677.2 12.5 %select_bitcast_fusion.5 = (f32[1,1024,192]{1,2,0:T(8,128)}, f32[1,1024,192]{1,2,0:T(8,128)}, f32[1,1024,192]{1,2,0:T(8,128)}, f32[1,1024,192]{1,2,0:T(8,128)}) fusion(f32[1024,192]{0,1:T(8,128)S(1)} %copy-done.14, pred[]{:T(512)S(6)} %eq.12, pred[]{:T(512)S(6)} %eq.14, f32[1024,192]{0,1:T(8,128)} %fusion.166, f32[1024,192]{0,1:T(8,128)} %fusion.164, ...), kind=kOutput, calls=%fused_computation.211 | convolution fusion | flops 4120969216 | bytes 18169860 | tf_op jit(solution)/shard_map/dot_general | solution.py:13
  689.7 2.4 maximum_select_fusion
  692.4 3.6 copy.49
  696.1 3.8 reshape.40
  700.1 1.4 copy-done.2
  701.9 4.0 fusion.124
  706.5 4.0 fusion.328
  710.7 15.8 %all_to_all.34 = f32[4,4,8192]{2,1,0:T(4,128)S(1)} all-to-all(f32[4,4,8192]{2,1,0:T(4,128)S(1)} %reshape.42), channel_id=1, replica_groups=mesh['fsdp'=8,'dp'=4] {'dp'}, dimensions={0} | all-to-all | bytes 1048576 | tf_op jit(solution)/shard_map/all_to_all | solution.py:139
  727.3 55.9 %all-reduce.5.cloned.1.call-done = f32[4,8192]{1,0:T(4,128)} async-done(((f32[4,8192]{1,0:T(4,128)}), f32[4,8192]{1,0:T(4,128)}) %all-reduce.5.cloned.1.call-update) | async-done | bytes 131088 | tf_op jit(solution)/shard_map/psum | solution.py:140
  785.4 13.4 %all-gather.4 = f32[32768]{0:T(1024)S(1)} all-gather(f32[8192]{0:T(1024)S(1)} %get-tuple-element.8), channel_id=6, replica_groups=mesh['fsdp'=8,'dp'=4] {'dp'}, dimensions={0}, use_global_device_ids=true | all-gather | bytes 163840 | tf_op jit(solution)/shard_map/all_gather | solution.py:142
  (112 shorter events, 25.1 us)
Async XLA Ops:
  7.2 14.8 %copy-start = (bf16[1024,1024]{1,0:T(8,128)(2,1)S(1)}, bf16[1024,1024]{1,0:T(8,128)(2,1)}, u32[]{:S(2)}) copy-start(bf16[1024,1024]{1,0:T(8,128)(2,1)} %param.11) | copy-start | bytes 6291460
  7.2 14.6 %copy-start.17 = (s32[1024,64]{0,1:T(8,128)S(1)}, s32[1024,64]{0,1:T(8,128)}, u32[]{:S(2)}) copy-start(s32[1024,64]{0,1:T(8,128)} %param.16) | copy-start | bytes 786436
  7.2 14.8 %copy-start.18 = (bf16[1024,128]{1,0:T(8,128)(2,1)S(1)}, bf16[1024,128]{1,0:T(8,128)(2,1)}, u32[]{:S(2)}) copy-start(bf16[1024,128]{1,0:T(8,128)(2,1)} %param.14) | copy-start | bytes 786436
  7.2 76.2 %all-reduce.3.cloned.1.call-start = ((), (), s32[]{:S(2)}) async-start(), calls=%async_computation.3 | async-start | bytes 1572864 | tf_op jit(solution)/shard_map/psum | solution.py:74
  13.7 44.5 %collective-permute-start = (bf16[1024,896]{1,0:T(8,128)(2,1)}, bf16[1024,896]{1,0:T(8,128)(2,1)}, u32[]{:S(2)}, u32[]{:S(2)}) collective-permute-start(bf16[1024,896]{1,0:T(8,128)(2,1)} %get-tuple-element.12), channel_id=1, source_target_pairs={{0,1},{3,2},{4,5},{7,6},{8,9},{11,10},{12,13},{15,14},{16,17},{19,... | collective-permute-start | bytes 5505032 | tf_op jit(solution)/shard_map/ppermute | solution.py:45
  19.8 38.3 %collective-permute-start.1 = (bf16[1024,896]{1,0:T(8,128)(2,1)}, bf16[1024,896]{1,0:T(8,128)(2,1)}, u32[]{:S(2)}, u32[]{:S(2)}) collective-permute-start(bf16[1024,896]{1,0:T(8,128)(2,1)} %get-tuple-element.12), channel_id=1, source_target_pairs={{1,2},{2,1},{5,6},{6,5},{9,10},{10,9},{13,14},{14,13},{17,18},{18,... | collective-permute-start | bytes 5505032 | tf_op jit(solution)/shard_map/ppermute | solution.py:46
  22.0 62.4 %copy-start.20 = (s32[128,128]{1,0:T(8,128)S(1)}, s32[128,128]{1,0:T(8,128)}, u32[]{:S(2)}) copy-start(s32[128,128]{1,0:T(8,128)} %param.19) | copy-start | bytes 196612
  58.2 33.5 %all-to-all-start = ((bf16[8,128,1024]{2,1,0:T(8,128)(2,1)}), bf16[8,128,1024]{2,1,0:T(8,128)(2,1)S(1)}, u32[]{:S(2)}, u32[]{:S(2)}) async-start(bf16[8,128,1024]{2,1,0:T(8,128)(2,1)} %bitcast.192), calls=%async_computation | async-start | bytes 4194304 | tf_op jit(solution)/shard_map/all_to_all | solution.py:54
  61.9 186.3 %all-gather.11.cloned.1.call-start = ((), (), s32[]{:S(2)}) async-start(), calls=%async_computation.4 | async-start | bytes 3932160 | tf_op jit(solution)/shard_map/all_gather | solution.py:81
  94.0 99.8 %all-to-all-start.1 = ((bf16[128,4,2048]{0,2,1:T(8,128)(2,1)}), bf16[128,4,2048]{0,2,1:T(8,128)(2,1)S(1)}, u32[]{:S(2)}, u32[]{:S(2)}) async-start(bf16[128,4,2048]{0,2,1:T(8,128)(2,1)} %bitcast.189), calls=%async_computation.1 | async-start | bytes 4194304 | tf_op jit(solution)/shard_map/all_to_all | solution.py:55
  100.1 146.6 %copy-start.13 = (s32[3584,64]{0,1:T(8,128)S(1)}, s32[3584,64]{0,1:T(8,128)}, u32[]{:S(2)}) copy-start(s32[3584,64]{0,1:T(8,128)} %param.17) | copy-start | bytes 2752516
  100.1 226.7 %all-gather.19.cloned.1.call-start = ((), (), s32[]{:S(2)}) async-start(), calls=%async_computation.9 | async-start | bytes 4718592 | tf_op jit(solution)/shard_map/all_gather | solution.py:60
  195.2 141.7 %all-gather.17.cloned.1.call-start = ((), (), s32[]{:S(2)}) async-start(), calls=%async_computation.8 | async-start | bytes 4718592 | tf_op jit(solution)/shard_map/all_gather | solution.py:60
  195.8 185.0 %all-gather.15.cloned.1.call-start = ((), (), s32[]{:S(2)}) async-start(), calls=%async_computation.7 | async-start | bytes 4718592 | tf_op jit(solution)/shard_map/all_gather | solution.py:60
  196.4 406.6 %all-gather.13.cloned.1.call-start = ((), (), s32[]{:S(2)}) async-start(), calls=%async_computation.6 | async-start | bytes 4718592 | tf_op jit(solution)/shard_map/all_gather | solution.py:60
  196.4 42.1 %collective-permute-start.3 = (bf16[1024,896]{1,0:T(8,128)(2,1)}, bf16[1024,896]{1,0:T(8,128)(2,1)}, u32[]{:S(2)}, u32[]{:S(2)}) collective-permute-start(bf16[1024,896]{1,0:T(8,128)(2,1)} %get-tuple-element.11), channel_id=1, source_target_pairs={{0,1},{3,2},{4,5},{7,6},{8,9},{11,10},{12,13},{15,14},{16,17},{19,... | collective-permute-start | bytes 5505032 | tf_op jit(solution)/shard_map/ppermute | solution.py:45
  198.9 45.2 %collective-permute-start.10 = (bf16[1024,896]{1,0:T(8,128)(2,1)}, bf16[1024,896]{1,0:T(8,128)(2,1)}, u32[]{:S(2)}, u32[]{:S(2)}) collective-permute-start(bf16[1024,896]{1,0:T(8,128)(2,1)} %get-tuple-element.11), channel_id=1, source_target_pairs={{1,2},{2,1},{5,6},{6,5},{9,10},{10,9},{13,14},{14,13},{17,18},{18,... | collective-permute-start | bytes 5505032 | tf_op jit(solution)/shard_map/ppermute | solution.py:46
  200.8 44.6 %collective-permute-start.16 = (bf16[1024,896]{1,0:T(8,128)(2,1)}, bf16[1024,896]{1,0:T(8,128)(2,1)}, u32[]{:S(2)}, u32[]{:S(2)}) collective-permute-start(bf16[1024,896]{1,0:T(8,128)(2,1)} %collective-permute-done), channel_id=1, source_target_pairs={{1,2},{2,1},{5,6},{6,5},{9,10},{10,9},{13,14},{14,13},{17,18},{18,... | collective-permute-start | bytes 5505032 | tf_op jit(solution)/shard_map/ppermute | solution.py:51
  202.7 51.5 %collective-permute-start.14 = (bf16[1024,896]{1,0:T(8,128)(2,1)}, bf16[1024,896]{1,0:T(8,128)(2,1)}, u32[]{:S(2)}, u32[]{:S(2)}) collective-permute-start(bf16[1024,896]{1,0:T(8,128)(2,1)} %get-tuple-element.10), channel_id=1, source_target_pairs={{1,2},{2,1},{5,6},{6,5},{9,10},{10,9},{13,14},{14,13},{17,18},{18,... | collective-permute-start | bytes 5505032 | tf_op jit(solution)/shard_map/ppermute | solution.py:46
  204.6 73.2 %collective-permute-start.7 = (bf16[1024,896]{1,0:T(8,128)(2,1)}, bf16[1024,896]{1,0:T(8,128)(2,1)}, u32[]{:S(2)}, u32[]{:S(2)}) collective-permute-start(bf16[1024,896]{1,0:T(8,128)(2,1)} %get-tuple-element.10), channel_id=1, source_target_pairs={{0,1},{3,2},{4,5},{7,6},{8,9},{11,10},{12,13},{15,14},{16,17},{19,... | collective-permute-start | bytes 5505032 | tf_op jit(solution)/shard_map/ppermute | solution.py:45
  238.5 77.1 %collective-permute-start.5 = (bf16[1024,896]{1,0:T(8,128)(2,1)}, bf16[1024,896]{1,0:T(8,128)(2,1)}, u32[]{:S(2)}, u32[]{:S(2)}) collective-permute-start(bf16[1024,896]{1,0:T(8,128)(2,1)} %get-tuple-element.13), channel_id=1, source_target_pairs={{0,1},{3,2},{4,5},{7,6},{8,9},{11,10},{12,13},{15,14},{16,17},{19,... | collective-permute-start | bytes 5505032 | tf_op jit(solution)/shard_map/ppermute | solution.py:45
  244.1 72.8 %collective-permute-start.9 = (bf16[1024,896]{1,0:T(8,128)(2,1)}, bf16[1024,896]{1,0:T(8,128)(2,1)}, u32[]{:S(2)}, u32[]{:S(2)}) collective-permute-start(bf16[1024,896]{1,0:T(8,128)(2,1)} %collective-permute-done.1), channel_id=1, source_target_pairs={{1,0},{2,3},{5,4},{6,7},{9,8},{10,11},{13,12},{14,15},{17,16},{18,... | collective-permute-start | bytes 5505032 | tf_op jit(solution)/shard_map/ppermute | solution.py:50
  245.4 79.2 %collective-permute-start.17 = (bf16[1024,896]{1,0:T(8,128)(2,1)}, bf16[1024,896]{1,0:T(8,128)(2,1)}, u32[]{:S(2)}, u32[]{:S(2)}) collective-permute-start(bf16[1024,896]{1,0:T(8,128)(2,1)} %collective-permute-done.16), channel_id=1, source_target_pairs={{1,0},{2,3},{5,4},{6,7},{9,8},{10,11},{13,12},{14,15},{17,16},{18,... | collective-permute-start | bytes 5505032 | tf_op jit(solution)/shard_map/ppermute | solution.py:52
  248.2 88.7 %copy-start.6 = (bf16[192,896]{1,0:T(8,128)(2,1)}, bf16[192,896]{1,0:T(8,128)(2,1)S(1)}, u32[]{:S(2)}) copy-start(bf16[192,896]{1,0:T(8,128)(2,1)S(1)} %get-tuple-element.27) | copy-start | bytes 1032196
  248.2 122.4 %copy-start.9 = (bf16[192,896]{1,0:T(8,128)(2,1)}, bf16[192,896]{1,0:T(8,128)(2,1)S(1)}, u32[]{:S(2)}) copy-start(bf16[192,896]{1,0:T(8,128)(2,1)S(1)} %get-tuple-element.26) | copy-start | bytes 1032196
  251.6 2.7 copy-start.5
  254.2 529.0 %all-reduce.5.cloned.1.call-start = ((), (), s32[]{:S(2)}) async-start(), calls=%async_computation.5 | async-start | bytes 262144 | tf_op jit(solution)/shard_map/psum | solution.py:140
  254.2 92.9 %collective-permute-start.12 = (bf16[1024,896]{1,0:T(8,128)(2,1)S(1)}, bf16[1024,896]{1,0:T(8,128)(2,1)}, u32[]{:S(2)}, u32[]{:S(2)}) collective-permute-start(bf16[1024,896]{1,0:T(8,128)(2,1)S(1)} %copy-done.5), channel_id=1, source_target_pairs={{1,2},{2,1},{5,6},{6,5},{9,10},{10,9},{13,14},{14,13},{17,18},{18,... | collective-permute-start | bytes 5505032 | tf_op jit(solution)/shard_map/ppermute | solution.py:46
  277.8 70.6 %collective-permute-start.18 = (bf16[1024,896]{1,0:T(8,128)(2,1)}, bf16[1024,896]{1,0:T(8,128)(2,1)}, u32[]{:S(2)}, u32[]{:S(2)}) collective-permute-start(bf16[1024,896]{1,0:T(8,128)(2,1)} %collective-permute-done.3), channel_id=1, source_target_pairs={{1,2},{2,1},{5,6},{6,5},{9,10},{10,9},{13,14},{14,13},{17,18},{18,... | collective-permute-start | bytes 5505032 | tf_op jit(solution)/shard_map/ppermute | solution.py:51
  315.6 50.9 %collective-permute-start.15 = (bf16[1024,896]{1,0:T(8,128)(2,1)}, bf16[1024,896]{1,0:T(8,128)(2,1)}, u32[]{:S(2)}, u32[]{:S(2)}) collective-permute-start(bf16[1024,896]{1,0:T(8,128)(2,1)} %collective-permute-done.14), channel_id=1, source_target_pairs={{1,0},{2,3},{5,4},{6,7},{9,8},{10,11},{13,12},{14,15},{17,16},{18,... | collective-permute-start | bytes 5505032 | tf_op jit(solution)/shard_map/ppermute | solution.py:50
  316.9 50.9 %collective-permute-start.22 = (bf16[1024,896]{1,0:T(8,128)(2,1)}, bf16[1024,896]{1,0:T(8,128)(2,1)}, u32[]{:S(2)}, u32[]{:S(2)}) collective-permute-start(bf16[1024,896]{1,0:T(8,128)(2,1)} %collective-permute-done.7), channel_id=1, source_target_pairs={{1,2},{2,1},{5,6},{6,5},{9,10},{10,9},{13,14},{14,13},{17,18},{18,... | collective-permute-start | bytes 5505032 | tf_op jit(solution)/shard_map/ppermute | solution.py:51
  324.6 44.5 %collective-permute-start.20 = (bf16[1024,896]{1,0:T(8,128)(2,1)}, bf16[1024,896]{1,0:T(8,128)(2,1)}, u32[]{:S(2)}, u32[]{:S(2)}) collective-permute-start(bf16[1024,896]{1,0:T(8,128)(2,1)} %collective-permute-done.5), channel_id=1, source_target_pairs={{1,2},{2,1},{5,6},{6,5},{9,10},{10,9},{13,14},{14,13},{17,18},{18,... | collective-permute-start | bytes 5505032 | tf_op jit(solution)/shard_map/ppermute | solution.py:51
  347.1 199.8 %collective-permute-start.11 = (bf16[1024,896]{1,0:T(8,128)(2,1)}, bf16[1024,896]{1,0:T(8,128)(2,1)}, u32[]{:S(2)}, u32[]{:S(2)}) collective-permute-start(bf16[1024,896]{1,0:T(8,128)(2,1)} %collective-permute-done.10), channel_id=1, source_target_pairs={{1,0},{2,3},{5,4},{6,7},{9,8},{10,11},{13,12},{14,15},{17,16},{18,... | collective-permute-start | bytes 5505032 | tf_op jit(solution)/shard_map/ppermute | solution.py:50
  348.4 226.0 %collective-permute-start.13 = (bf16[1024,896]{1,0:T(8,128)(2,1)}, bf16[1024,896]{1,0:T(8,128)(2,1)}, u32[]{:S(2)}, u32[]{:S(2)}) collective-permute-start(bf16[1024,896]{1,0:T(8,128)(2,1)} %collective-permute-done.12), channel_id=1, source_target_pairs={{1,0},{2,3},{5,4},{6,7},{9,8},{10,11},{13,12},{14,15},{17,16},{18,... | collective-permute-start | bytes 5505032 | tf_op jit(solution)/shard_map/ppermute | solution.py:50
  366.5 118.0 %collective-permute-start.19 = (bf16[1024,896]{1,0:T(8,128)(2,1)}, bf16[1024,896]{1,0:T(8,128)(2,1)}, u32[]{:S(2)}, u32[]{:S(2)}) collective-permute-start(bf16[1024,896]{1,0:T(8,128)(2,1)} %collective-permute-done.18), channel_id=1, source_target_pairs={{1,0},{2,3},{5,4},{6,7},{9,8},{10,11},{13,12},{14,15},{17,16},{18,... | collective-permute-start | bytes 5505032 | tf_op jit(solution)/shard_map/ppermute | solution.py:52
  367.8 156.0 %collective-permute-start.23 = (bf16[1024,896]{1,0:T(8,128)(2,1)}, bf16[1024,896]{1,0:T(8,128)(2,1)}, u32[]{:S(2)}, u32[]{:S(2)}) collective-permute-start(bf16[1024,896]{1,0:T(8,128)(2,1)} %collective-permute-done.22), channel_id=1, source_target_pairs={{1,0},{2,3},{5,4},{6,7},{9,8},{10,11},{13,12},{14,15},{17,16},{18,... | collective-permute-start | bytes 5505032 | tf_op jit(solution)/shard_map/ppermute | solution.py:52
  369.1 218.7 %collective-permute-start.21 = (bf16[1024,896]{1,0:T(8,128)(2,1)}, bf16[1024,896]{1,0:T(8,128)(2,1)}, u32[]{:S(2)}, u32[]{:S(2)}) collective-permute-start(bf16[1024,896]{1,0:T(8,128)(2,1)} %collective-permute-done.20), channel_id=1, source_target_pairs={{1,0},{2,3},{5,4},{6,7},{9,8},{10,11},{13,12},{14,15},{17,16},{18,... | collective-permute-start | bytes 5505032 | tf_op jit(solution)/shard_map/ppermute | solution.py:52
  380.8 10.2 %copy-start.22 = (bf16[1024,1,2048]{0,2,1:T(8,128)(2,1)S(1)}, bf16[1024,1,2048]{0,2,1:T(8,128)(2,1)}, u32[]{:S(2)}) copy-start(bf16[1024,1,2048]{0,2,1:T(8,128)(2,1)} %all-gather.15.cloned.1.call-done) | copy-start | bytes 12582916
  484.5 118.5 %collective-permute-start.4 = (bf16[1024,896]{1,0:T(8,128)(2,1)}, bf16[1024,896]{1,0:T(8,128)(2,1)}, u32[]{:S(2)}, u32[]{:S(2)}) collective-permute-start(bf16[1024,896]{1,0:T(8,128)(2,1)} %fusion.101), channel_id=1, source_target_pairs={{0,1},{3,2},{4,5},{7,6},{8,9},{11,10},{12,13},{15,14},{16,17},{19,... | collective-permute-start | bytes 5505032 | tf_op jit(solution)/shard_map/ppermute | solution.py:102
  512.4 14.2 %copy-start.10 = (bf16[192,896]{1,0:T(8,128)(2,1)S(1)}, bf16[192,896]{1,0:T(8,128)(2,1)}, u32[]{:S(2)}) copy-start(bf16[192,896]{1,0:T(8,128)(2,1)} %copy-done.9) | copy-start | bytes 1032196
  523.8 90.2 %collective-permute-start.6 = (bf16[1024,896]{1,0:T(8,128)(2,1)S(1)}, bf16[1024,896]{1,0:T(8,128)(2,1)}, u32[]{:S(2)}, u32[]{:S(2)}) collective-permute-start(bf16[1024,896]{1,0:T(8,128)(2,1)S(1)} %fusion.102), channel_id=1, source_target_pairs={{0,1},{3,2},{4,5},{7,6},{8,9},{11,10},{12,13},{15,14},{16,17},{19,... | collective-permute-start | bytes 5505032 | tf_op jit(solution)/shard_map/ppermute | solution.py:102
  536.8 12.9 %copy-start.23 = (f32[1024,192]{0,1:T(8,128)S(1)}, f32[1024,192]{0,1:T(8,128)}, u32[]{:S(2)}) copy-start(f32[1024,192]{0,1:T(8,128)} %fusion.144) | copy-start | bytes 2359300
  546.9 130.3 %collective-permute-start.2 = (bf16[1024,896]{1,0:T(8,128)(2,1)}, bf16[1024,896]{1,0:T(8,128)(2,1)}, u32[]{:S(2)}, u32[]{:S(2)}) collective-permute-start(bf16[1024,896]{1,0:T(8,128)(2,1)} %fusion.100), channel_id=1, source_target_pairs={{0,1},{3,2},{4,5},{7,6},{8,9},{11,10},{12,13},{15,14},{16,17},{19,... | collective-permute-start | bytes 5505032 | tf_op jit(solution)/shard_map/ppermute | solution.py:102
  559.7 10.1 %copy-start.7 = (bf16[192,896]{1,0:T(8,128)(2,1)S(1)}, bf16[192,896]{1,0:T(8,128)(2,1)}, u32[]{:S(2)}) copy-start(bf16[192,896]{1,0:T(8,128)(2,1)} %copy-done.6) | copy-start | bytes 1032196
  574.4 91.8 %collective-permute-start.8 = (bf16[1024,896]{1,0:T(8,128)(2,1)}, bf16[1024,896]{1,0:T(8,128)(2,1)}, u32[]{:S(2)}, u32[]{:S(2)}) collective-permute-start(bf16[1024,896]{1,0:T(8,128)(2,1)} %fusion.103), channel_id=1, source_target_pairs={{0,1},{3,2},{4,5},{7,6},{8,9},{11,10},{12,13},{15,14},{16,17},{19,... | collective-permute-start | bytes 5505032 | tf_op jit(solution)/shard_map/ppermute | solution.py:102
  598.8 1.0 copy-start.11
  613.9 52.3 %copy-start.12 = (bf16[192,896]{1,0:T(8,128)(2,1)S(1)}, bf16[192,896]{1,0:T(8,128)(2,1)}, u32[]{:S(2)}) copy-start(bf16[192,896]{1,0:T(8,128)(2,1)} %copy-done.9) | copy-start | bytes 1032196
  624.7 52.4 %copy-start.8 = (bf16[192,896]{1,0:T(8,128)(2,1)S(1)}, bf16[192,896]{1,0:T(8,128)(2,1)}, u32[]{:S(2)}) copy-start(bf16[192,896]{1,0:T(8,128)(2,1)} %copy-done.6) | copy-start | bytes 1032196
  624.7 52.5 %copy-start.14 = (f32[1024,192]{0,1:T(8,128)S(1)}, f32[1024,192]{0,1:T(8,128)}, u32[]{:S(2)}) copy-start(f32[1024,192]{0,1:T(8,128)} %fusion.264) | copy-start | bytes 2359300
  677.2 12.5 %copy-start.15 = (f32[1,1024,192]{1,2,0:T(8,128)S(1)}, f32[1,1024,192]{1,2,0:T(8,128)}, u32[]{:S(2)}) copy-start(f32[1,1024,192]{1,2,0:T(8,128)} %get-tuple-element.24) | copy-start | bytes 2359300
  677.2 12.5 %copy-start.16 = (f32[1,1024,192]{1,2,0:T(8,128)S(1)}, f32[1,1024,192]{1,2,0:T(8,128)}, u32[]{:S(2)}) copy-start(f32[1,1024,192]{1,2,0:T(8,128)} %get-tuple-element.25) | copy-start | bytes 2359300
  699.9 1.6 copy-start.2
  699.9 2.0 copy-start.4
  701.5 4.4 copy-start.21
  701.5 5.0 copy-start.3
  701.9 4.6 slice-start
  705.9 95.5 %copy-start.1 = (bf16[1024,1024]{1,0:T(8,128)(2,1)S(1)}, bf16[1024,1024]{1,0:T(8,128)(2,1)}, u32[]{:S(2)}) copy-start(bf16[1024,1024]{1,0:T(8,128)(2,1)} %param.11) | copy-start | bytes 6291460
  785.3 16.1 %copy-start.19 = (f32[4,8192]{1,0:T(4,128)}, f32[4,8192]{1,0:T(4,128)S(1)}, u32[]{:S(2)}) copy-start(f32[4,8192]{1,0:T(4,128)S(1)} %get-tuple-element.9) | copy-start | bytes 393220
Sparse Core Ops, SparseCore 0:
  23.9 59.4 all-reduce.2
  86.9 109.4 all-gather.10
  198.2 35.9 all-gather.18
  236.0 37.4 all-gather.16
  275.2 37.4 all-gather.14
  314.4 37.4 all-gather.12
  727.4 55.7 all-reduce.4

commit v3 on v2

--- a/solution.py
+++ b/solution.py
@@ -6,7 +6,7 @@
 K1 = 64
 K2 = 128
 SEQ = 256
-CHUNKS = 4
+CHUNKS = 2
 
 
 def contract_last(left, right):

time: 815 us -> 797 us (0.978)
  starting transfers between devices: 91.1 us -> 202 us
  waiting for transfers between devices: 449 us -> 356 us
  matrix products: 187 us -> 151 us
    ppermute x4 -> x2, starting transfers between devices: 36.5 us -> 167 us  [body(): neighbour.append(lax.ppermute(scaled, 'dp', inward))]
    ppermute x4 -> x2, waiting for transfers between devices: 41.5 us -> 0.01 us  [body(): neighbour.append(lax.ppermute(scaled, 'dp', inward))]
    ppermute x4 -> x2, waiting for transfers between devices: 92.4 us -> 55.5 us  [body(): last_outer = [lax.ppermute(v, 'dp', outward) for v in last_inner]]
    dot_general x20 -> x10, matrix products: 174 us -> 138 us  [contract_last(): lax.dot_general(left, right, (((1,), (1,)), ((), ())), preferred_element_...]
    ppermute x4 -> x2, waiting for transfers between devices: 122 us -> 145 us  [body(): near = [lax.ppermute(v, 'dp', inward) for v in own]]
    psum x1, waiting for transfers between devices: 21.5 us -> 0.02 us  [body(): model_side = lax.psum(model_side, 'fsdp')]
    all_to_all x1, waiting for transfers between devices: 4.91 us -> 23.3 us  [body(): rows = lax.all_to_all(grad_out, 'fsdp', 0, 1, tiled=True)]
    ppermute x4 -> x2, waiting for transfers between devices: 16.8 us -> 0.01 us  [body(): far_outer = [lax.ppermute(v, 'dp', outward) for v in far_inner]]
  transfers between devices with their start and end apart: 33 -> 21, of which waited for: 13 -> 6; matrix products, arithmetic and copies ran while one was open for 22% -> 17% of each run, Pallas kernels for 0% -> 0%
where the time goes in v3:
time: 797 us; the launch traced here: 789 us
  waiting for transfers between devices  356 us (45%)
  starting transfers between devices  202 us (25%)
  matrix products  151 us (19%)
  blocking collectives  29.6 us (4%)
  local copies, waits for them, and re-layouts  27 us (3%)
  between operations  15.4 us (2%)
  other arithmetic  8.21 us (1%)
    ppermute x2, starting transfers between devices, body(): neighbour.append(lax.ppermute(scaled, 'dp', inward))  167 us
    ppermute x2, waiting for transfers between devices, body(): near = [lax.ppermute(v, 'dp', inward) for v in own]  145 us
    dot_general x10, matrix products, contract_last(): lax.dot_general(left, right, (((1,), (1,)), ((), ())), preferred_element_...  138 us
    all_to_all x1, waiting for transfers between devices, body(): rows = lax.all_to_all(rows, 'dp', 1, 0, tiled=True)  78.8 us
    ppermute x2, waiting for transfers between devices, body(): last_outer = [lax.ppermute(v, 'dp', outward) for v in last_inner]  55.5 us
    psum x1, waiting for transfers between devices, body(): projected = lax.psum(jnp.sum(projected, axis=0), 'fsdp')  53.3 us
    all_to_all x1, waiting for transfers between devices, body(): rows = lax.all_to_all(grad_out, 'fsdp', 0, 1, tiled=True)  23.3 us
    all_to_all x1, blocking collectives, body(): projected = lax.all_to_all(projected, 'dp', 0, 0, tiled=True)  16.2 us
  transfers between devices with their start and end apart: 21, of which 6 were waited for; matrix products, arithmetic and copies ran while one was open for 17% of the time, Pallas kernels for 0%

profile of v3, /device:TPU:0, one launch (start us, length us, event | category | flops | bytes accessed | tf_op | source)
XLA Modules:
  0.0 789.1 jit_solution(15888073084001146205)
XLA Ops:
  7.2 6.7 fusion.179
  13.9 6.7 collective-permute-start
  20.6 2.4 collective-permute-start.1
  23.1 0.2 copy.51
  23.3 1.8 convolution_bitcast_fusion
  25.2 72.6 %collective-permute-done = bf16[1024,1792]{1,0:T(8,128)(2,1)} collective-permute-done((bf16[1024,1792]{1,0:T(8,128)(2,1)}, bf16[1024,1792]{1,0:T(8,128)(2,1)}, u32[]{:S(2)}, u32[]{:S(2)}) %collective-permute-start) | collective-permute-done | bytes 3670048 | tf_op jit(solution)/shard_map/ppermute | solution.py:45
  97.7 3.7 all-to-all-start
  101.5 1.0 slice.65
  102.5 1.3 fusion.162
  103.8 1.0 pad_maximum_fusion.2
  104.8 23.3 %all-to-all-done = bf16[8,128,1024]{2,1,0:T(8,128)(2,1)S(1)} async-done(((bf16[8,128,1024]{2,1,0:T(8,128)(2,1)}), bf16[8,128,1024]{2,1,0:T(8,128)(2,1)S(1)}, u32[]{:S(2)}, u32[]{:S(2)}) %all-to-all-start) | async-done | bytes 2097184 | tf_op jit(solution)/shard_map/all_to_all | solution.py:54
  128.1 2.5 copy.44
  130.6 6.2 all-to-all-start.1
  136.8 78.8 %all-to-all-done.1 = bf16[128,4,2048]{0,2,1:T(8,128)(2,1)S(1)} async-done(((bf16[128,4,2048]{0,2,1:T(8,128)(2,1)}), bf16[128,4,2048]{0,2,1:T(8,128)(2,1)S(1)}, u32[]{:S(2)}, u32[]{:S(2)}) %all-to-all-start.1) | async-done | bytes 2097184 | tf_op jit(solution)/shard_map/all_to_all | solution.py:55
  215.6 1.4 constant_dynamic-slice_fusion.1
  217.0 0.0 all-gather.17.cloned.1.call-start
  217.0 0.5 all-gather.17.cloned.1.call-update
  217.6 3.1 collective-permute-start.3
  220.7 0.0 all-gather.13.cloned.1.call-start
  220.8 2.5 collective-permute-start.6
  223.3 2.6 collective-permute-start.8
  225.8 72.2 %collective-permute-done.3 = bf16[1024,1792]{1,0:T(8,128)(2,1)} collective-permute-done((bf16[1024,1792]{1,0:T(8,128)(2,1)}, bf16[1024,1792]{1,0:T(8,128)(2,1)}, u32[]{:S(2)}, u32[]{:S(2)}) %collective-permute-start.3) | collective-permute-done | bytes 3670048 | tf_op jit(solution)/shard_map/ppermute | solution.py:45
  298.0 2.6 collective-permute-start.10
  300.7 1.3 pad_maximum_fusion.3
  302.0 1.3 collective-permute-start.5
  303.3 1.3 collective-permute-start.7
  304.6 3.1 copy.59
  307.7 1.1 slice.67
  308.8 1.5 slice.66
  310.3 1.3 collective-permute-start.9
  311.6 1.3 collective-permute-start.11
  313.0 15.3 %fusion.35 = bf16[1024,1792]{1,0:T(8,128)(2,1)} fusion(bf16[1024,1792]{1,0:T(8,128)(2,1)} %collective-permute-done.3, bf16[3584,2048]{1,0:T(8,128)(2,1)} %param.13, bf16[1024,1,2048]{0,2,1:T(8,128)(2,1)} %all-gather.15.cloned.1.call-done, pred[]{:T(512)S(6)} %or.3), kind=kOutput, calls=%fused_computation.53 | convolution fusion | flops 7530872832 | bytes 18874368 | tf_op jit(solution)/shard_map/dot_general | solution.py:13
  328.4 163.5 %collective-permute-start.4 = (bf16[1024,1792]{1,0:T(8,128)(2,1)}, bf16[1024,1792]{1,0:T(8,128)(2,1)}, u32[]{:S(2)}, u32[]{:S(2)}) collective-permute-start(bf16[1024,1792]{1,0:T(8,128)(2,1)} %fusion.35), channel_id=1, source_target_pairs={{0,1},{3,2},{4,5},{7,6},{8,9},{11,10},{12,13},{15,14},{16,17},{19,... | collective-permute-start | bytes 11010056 | tf_op jit(solution)/shard_map/ppermute | solution.py:102
  491.9 14.1 %fusion.34 = bf16[1024,1792]{1,0:T(8,128)(2,1)} fusion(bf16[1024,1792]{1,0:T(8,128)(2,1)} %collective-permute-done, bf16[3584,2048]{1,0:T(8,128)(2,1)} %param.13, bf16[1024,1,2048]{0,2,1:T(8,128)(2,1)S(1)} %copy-done.12, pred[]{:T(512)S(6)} %or.3), kind=kOutput, calls=%fused_computation.52 | convolution fusion | flops 7530872832 | bytes 18874368 | tf_op jit(solution)/shard_map/dot_general | solution.py:13
  506.0 3.4 fusion.192
  509.4 4.3 fusion.151
  513.6 3.1 collective-permute-start.2
  516.7 15.6 %fusion.66 = f32[1024,192]{0,1:T(8,128)S(1)} fusion(bf16[192,1792]{1,0:T(8,128)(2,1)S(1)} %get-tuple-element.25, bf16[1024,1792]{1,0:T(8,128)(2,1)} %collective-permute-done.5, bf16[1024,1792]{1,0:T(8,128)(2,1)} %collective-permute-done.1, pred[]{:T(512)S(6)} %or.3, bf16[3584,2048]{1,0:T(8,128)(2,1)} %param.13, ...), kind=kOutput, calls=%fused_computation.80 | convolution fusion | flops 8235515904 | bytes 20348928 | tf_op jit(solution)/shard_map/dot_general | solution.py:13
  532.3 16.0 %fusion.144 = f32[1024,192]{0,1:T(8,128)S(1)} fusion(f32[1024,192]{0,1:T(8,128)S(1)} %fusion.66, bf16[192,1792]{1,0:T(8,128)(2,1)S(1)} %get-tuple-element.24, bf16[1024,1792]{1,0:T(8,128)(2,1)} %collective-permute-done.7, bf16[1024,1792]{1,0:T(8,128)(2,1)} %collective-permute-done.6, pred[]{:T(512)S(6)} %or.3, bf16[3584,2048]{1,0:T(8,128)(2,1)} %param.13, ...), kind=kOutput, calls=%fused_computation.100 | convolution fusion | flops 8235712512 | bytes 21135360 | tf_op jit(solution)/shard_map/dot_general | solution.py:13
  548.4 16.7 %fusion.70 = f32[1024,192]{0,1:T(8,128)} fusion(bf16[192,1792]{1,0:T(8,128)(2,1)S(1)} %get-tuple-element.25, bf16[1024,1792]{1,0:T(8,128)(2,1)} %collective-permute-done.9, bf16[1024,1792]{1,0:T(8,128)(2,1)} %collective-permute-done.8, pred[]{:T(512)S(6)} %or.3, bf16[3584,2048]{1,0:T(8,128)(2,1)} %param.13, ...), kind=kOutput, calls=%fused_computation.82 | convolution fusion | flops 8235515904 | bytes 20348928 | tf_op jit(solution)/shard_map/dot_general | solution.py:13
  565.1 55.5 %collective-permute-done.11 = bf16[1024,1792]{1,0:T(8,128)(2,1)} collective-permute-done((bf16[1024,1792]{1,0:T(8,128)(2,1)}, bf16[1024,1792]{1,0:T(8,128)(2,1)}, u32[]{:S(2)}, u32[]{:S(2)}) %collective-permute-start.11) | collective-permute-done | bytes 3670048 | tf_op jit(solution)/shard_map/ppermute | solution.py:52
  620.6 16.0 %select_bitcast_fusion.3 = (f32[1,1024,192]{1,2,0:T(8,128)S(1)}, f32[1,1024,192]{1,2,0:T(8,128)S(1)}) fusion(f32[1024,192]{0,1:T(8,128)S(1)} %fusion.144, pred[]{:T(512)S(6)} %lt.13, f32[1024,192]{0,1:T(8,128)} %fusion.70, bf16[192,1792]{1,0:T(8,128)(2,1)S(1)} %get-tuple-element.24, bf16[1024,1792]{1,0:T(8,128)(2,1)} %collective-permute-done.11, ...), kind=kOutput, calls=%fused_computation.111 | convolution fusion | flops 8236105728 | bytes 22708226 | tf_op jit(solution)/shard_map/dot_general | solution.py:13
  636.6 17.6 %fusion.76 = f32[1024,192]{0,1:T(8,128)} fusion(bf16[192,1792]{1,0:T(8,128)(2,1)S(1)} %get-tuple-element.24, bf16[1024,1792]{1,0:T(8,128)(2,1)} %collective-permute-done.4, pred[]{:T(512)S(6)} %or.3, bf16[3584,2048]{1,0:T(8,128)(2,1)} %param.13, bf16[1024,1,2048]{0,2,1:T(8,128)(2,1)} %all-gather.13.cloned.1.call-done, bf16[1024,3584]{1,0:T(8,128)(2,1)} %param.12), kind=kOutput, calls=%fused_computation.85 | convolution fusion | flops 8239185920 | bytes 20348928 | tf_op jit(solution)/shard_map/dot_general | solution.py:13
  654.2 18.9 %select_bitcast_fusion.5 = (f32[1,1024,192]{1,2,0:T(8,128)S(1)}, f32[1,1024,192]{1,2,0:T(8,128)S(1)}, f32[1,1024,192]{1,2,0:T(8,128)}, f32[1,1024,192]{1,2,0:T(8,128)}) fusion(f32[1024,192]{0,1:T(8,128)} %fusion.151, pred[]{:T(512)S(6)} %eq.12, pred[]{:T(512)S(6)} %eq.14, f32[1024,192]{0,1:T(8,128)} %fusion.76, bf16[192,1792]{1,0:T(8,128)(2,1)} %copy-done.6, ...), kind=kOutput, calls=%fused_computation.113 | convolution fusion | flops 8240168960 | bytes 24281092 | tf_op jit(solution)/shard_map/dot_general | solution.py:13
  673.2 1.8 maximum_select_fusion
  675.0 0.4 pad_maximum_fusion
  675.4 3.7 copy.49
  679.0 3.7 reshape.40
  682.8 0.2 slice.68
  682.9 1.4 copy-done.2
  684.4 0.4 copy-done.4
  684.8 4.0 fusion.126
  688.8 0.6 fusion.163
  689.4 4.0 fusion.152
  693.4 0.2 reshape.42
  693.6 16.2 %all_to_all.34 = f32[4,4,8192]{2,1,0:T(4,128)S(1)} all-to-all(f32[4,4,8192]{2,1,0:T(4,128)S(1)} %reshape.42), channel_id=1, replica_groups=mesh['fsdp'=8,'dp'=4] {'dp'}, dimensions={0} | all-to-all | bytes 1048576 | tf_op jit(solution)/shard_map/all_to_all | solution.py:139
  709.8 0.8 reduce_sum.45
  710.5 53.3 %all-reduce.5.cloned.1.call-done = f32[4,8192]{1,0:T(4,128)} async-done(((f32[4,8192]{1,0:T(4,128)}), f32[4,8192]{1,0:T(4,128)}) %all-reduce.5.cloned.1.call-update) | async-done | bytes 131088 | tf_op jit(solution)/shard_map/psum | solution.py:140
  763.8 1.1 multiply_reduce_fusion
  764.9 1.1 fusion.178
  766.0 13.4 %all-gather.4 = f32[32768]{0:T(1024)S(1)} all-gather(f32[8192]{0:T(1024)S(1)} %get-tuple-element.8), channel_id=6, replica_groups=mesh['fsdp'=8,'dp'=4] {'dp'}, dimensions={0}, use_global_device_ids=true | all-gather | bytes 163840 | tf_op jit(solution)/shard_map/all_gather | solution.py:142
  779.5 0.1 reduce_sum.48
  779.6 0.6 multiply_reduce_fusion.1
  780.9 1.2 fusion.155
  (56 shorter events, 0.6 us)
Async XLA Ops:
  7.2 16.1 %copy-start = (bf16[1024,1024]{1,0:T(8,128)(2,1)S(1)}, bf16[1024,1024]{1,0:T(8,128)(2,1)}, u32[]{:S(2)}) copy-start(bf16[1024,1024]{1,0:T(8,128)(2,1)} %param.11) | copy-start | bytes 6291460
  7.2 15.9 %copy-start.7 = (s32[1024,64]{0,1:T(8,128)S(1)}, s32[1024,64]{0,1:T(8,128)}, u32[]{:S(2)}) copy-start(s32[1024,64]{0,1:T(8,128)} %param.16) | copy-start | bytes 786436
  7.2 16.1 %copy-start.8 = (bf16[1024,128]{1,0:T(8,128)(2,1)S(1)}, bf16[1024,128]{1,0:T(8,128)(2,1)}, u32[]{:S(2)}) copy-start(bf16[1024,128]{1,0:T(8,128)(2,1)} %param.14) | copy-start | bytes 786436
  7.2 94.3 %all-reduce.3.cloned.1.call-start = ((), (), s32[]{:S(2)}) async-start(), calls=%async_computation.3 | async-start | bytes 1572864 | tf_op jit(solution)/shard_map/psum | solution.py:74
  13.9 83.8 %collective-permute-start = (bf16[1024,1792]{1,0:T(8,128)(2,1)}, bf16[1024,1792]{1,0:T(8,128)(2,1)}, u32[]{:S(2)}, u32[]{:S(2)}) collective-permute-start(bf16[1024,1792]{1,0:T(8,128)(2,1)} %get-tuple-element.11), channel_id=1, source_target_pairs={{0,1},{3,2},{4,5},{7,6},{8,9},{11,10},{12,13},{15,14},{16,17},{19,... | collective-permute-start | bytes 11010056 | tf_op jit(solution)/shard_map/ppermute | solution.py:45
  20.6 77.1 %collective-permute-start.1 = (bf16[1024,1792]{1,0:T(8,128)(2,1)}, bf16[1024,1792]{1,0:T(8,128)(2,1)}, u32[]{:S(2)}, u32[]{:S(2)}) collective-permute-start(bf16[1024,1792]{1,0:T(8,128)(2,1)} %get-tuple-element.11), channel_id=1, source_target_pairs={{1,2},{2,1},{5,6},{6,5},{9,10},{10,9},{13,14},{14,13},{17,18},{18,... | collective-permute-start | bytes 11010056 | tf_op jit(solution)/shard_map/ppermute | solution.py:46
  23.3 79.2 %copy-start.10 = (s32[128,128]{1,0:T(8,128)S(1)}, s32[128,128]{1,0:T(8,128)}, u32[]{:S(2)}) copy-start(s32[128,128]{1,0:T(8,128)} %param.19) | copy-start | bytes 196612
  97.7 30.4 %all-to-all-start = ((bf16[8,128,1024]{2,1,0:T(8,128)(2,1)}), bf16[8,128,1024]{2,1,0:T(8,128)(2,1)S(1)}, u32[]{:S(2)}, u32[]{:S(2)}) async-start(bf16[8,128,1024]{2,1,0:T(8,128)(2,1)} %bitcast.114), calls=%async_computation | async-start | bytes 4194304 | tf_op jit(solution)/shard_map/all_to_all | solution.py:54
  101.5 203.2 %all-gather.11.cloned.1.call-start = ((), (), s32[]{:S(2)}) async-start(), calls=%async_computation.4 | async-start | bytes 3932160 | tf_op jit(solution)/shard_map/all_gather | solution.py:81
  130.6 170.0 %copy-start.5 = (s32[3584,64]{0,1:T(8,128)S(1)}, s32[3584,64]{0,1:T(8,128)}, u32[]{:S(2)}) copy-start(s32[3584,64]{0,1:T(8,128)} %param.17) | copy-start | bytes 2752516
  130.6 85.0 %all-to-all-start.1 = ((bf16[128,4,2048]{0,2,1:T(8,128)(2,1)}), bf16[128,4,2048]{0,2,1:T(8,128)(2,1)S(1)}, u32[]{:S(2)}, u32[]{:S(2)}) async-start(bf16[128,4,2048]{0,2,1:T(8,128)(2,1)} %bitcast.111), calls=%async_computation.1 | async-start | bytes 4194304 | tf_op jit(solution)/shard_map/all_to_all | solution.py:55
  136.8 176.3 %all-gather.15.cloned.1.call-start = ((), (), s32[]{:S(2)}) async-start(), calls=%async_computation.7 | async-start | bytes 4718592 | tf_op jit(solution)/shard_map/all_gather | solution.py:60
  217.0 299.7 %all-gather.17.cloned.1.call-start = ((), (), s32[]{:S(2)}) async-start(), calls=%async_computation.8 | async-start | bytes 4718592 | tf_op jit(solution)/shard_map/all_gather | solution.py:60
  217.6 330.8 %all-gather.19.cloned.1.call-start = ((), (), s32[]{:S(2)}) async-start(), calls=%async_computation.9 | async-start | bytes 4718592 | tf_op jit(solution)/shard_map/all_gather | solution.py:60
  217.6 80.4 %collective-permute-start.3 = (bf16[1024,1792]{1,0:T(8,128)(2,1)}, bf16[1024,1792]{1,0:T(8,128)(2,1)}, u32[]{:S(2)}, u32[]{:S(2)}) collective-permute-start(bf16[1024,1792]{1,0:T(8,128)(2,1)} %get-tuple-element.10), channel_id=1, source_target_pairs={{0,1},{3,2},{4,5},{7,6},{8,9},{11,10},{12,13},{15,14},{16,17},{19,... | collective-permute-start | bytes 11010056 | tf_op jit(solution)/shard_map/ppermute | solution.py:45
  220.7 415.9 %all-gather.13.cloned.1.call-start = ((), (), s32[]{:S(2)}) async-start(), calls=%async_computation.6 | async-start | bytes 4718592 | tf_op jit(solution)/shard_map/all_gather | solution.py:60
  220.8 82.5 %collective-permute-start.6 = (bf16[1024,1792]{1,0:T(8,128)(2,1)}, bf16[1024,1792]{1,0:T(8,128)(2,1)}, u32[]{:S(2)}, u32[]{:S(2)}) collective-permute-start(bf16[1024,1792]{1,0:T(8,128)(2,1)} %get-tuple-element.10), channel_id=1, source_target_pairs={{1,2},{2,1},{5,6},{6,5},{9,10},{10,9},{13,14},{14,13},{17,18},{18,... | collective-permute-start | bytes 11010056 | tf_op jit(solution)/shard_map/ppermute | solution.py:46
  223.3 87.1 %collective-permute-start.8 = (bf16[1024,1792]{1,0:T(8,128)(2,1)}, bf16[1024,1792]{1,0:T(8,128)(2,1)}, u32[]{:S(2)}, u32[]{:S(2)}) collective-permute-start(bf16[1024,1792]{1,0:T(8,128)(2,1)} %collective-permute-done), channel_id=1, source_target_pairs={{1,2},{2,1},{5,6},{6,5},{9,10},{10,9},{13,14},{14,13},{17,18},{18,... | collective-permute-start | bytes 11010056 | tf_op jit(solution)/shard_map/ppermute | solution.py:51
  298.0 13.6 %collective-permute-start.10 = (bf16[1024,1792]{1,0:T(8,128)(2,1)}, bf16[1024,1792]{1,0:T(8,128)(2,1)}, u32[]{:S(2)}, u32[]{:S(2)}) collective-permute-start(bf16[1024,1792]{1,0:T(8,128)(2,1)} %collective-permute-done.3), channel_id=1, source_target_pairs={{1,2},{2,1},{5,6},{6,5},{9,10},{10,9},{13,14},{14,13},{17,18},{18,... | collective-permute-start | bytes 11010056 | tf_op jit(solution)/shard_map/ppermute | solution.py:51
  302.0 246.4 %copy-start.6 = (bf16[192,1792]{1,0:T(8,128)(2,1)}, bf16[192,1792]{1,0:T(8,128)(2,1)S(1)}, u32[]{:S(2)}) copy-start(bf16[192,1792]{1,0:T(8,128)(2,1)S(1)} %get-tuple-element.25) | copy-start | bytes 2064388
  302.0 211.6 %collective-permute-start.5 = (bf16[1024,1792]{1,0:T(8,128)(2,1)}, bf16[1024,1792]{1,0:T(8,128)(2,1)}, u32[]{:S(2)}, u32[]{:S(2)}) collective-permute-start(bf16[1024,1792]{1,0:T(8,128)(2,1)} %collective-permute-done.1), channel_id=1, source_target_pairs={{1,0},{2,3},{5,4},{6,7},{9,8},{10,11},{13,12},{14,15},{17,16},{18,... | collective-permute-start | bytes 11010056 | tf_op jit(solution)/shard_map/ppermute | solution.py:50
  303.3 229.0 %collective-permute-start.7 = (bf16[1024,1792]{1,0:T(8,128)(2,1)}, bf16[1024,1792]{1,0:T(8,128)(2,1)}, u32[]{:S(2)}, u32[]{:S(2)}) collective-permute-start(bf16[1024,1792]{1,0:T(8,128)(2,1)} %collective-permute-done.6), channel_id=1, source_target_pairs={{1,0},{2,3},{5,4},{6,7},{9,8},{10,11},{13,12},{14,15},{17,16},{18,... | collective-permute-start | bytes 11010056 | tf_op jit(solution)/shard_map/ppermute | solution.py:50
  310.3 238.0 %collective-permute-start.9 = (bf16[1024,1792]{1,0:T(8,128)(2,1)}, bf16[1024,1792]{1,0:T(8,128)(2,1)}, u32[]{:S(2)}, u32[]{:S(2)}) collective-permute-start(bf16[1024,1792]{1,0:T(8,128)(2,1)} %collective-permute-done.8), channel_id=1, source_target_pairs={{1,0},{2,3},{5,4},{6,7},{9,8},{10,11},{13,12},{14,15},{17,16},{18,... | collective-permute-start | bytes 11010056 | tf_op jit(solution)/shard_map/ppermute | solution.py:52
  311.6 309.0 %collective-permute-start.11 = (bf16[1024,1792]{1,0:T(8,128)(2,1)}, bf16[1024,1792]{1,0:T(8,128)(2,1)}, u32[]{:S(2)}, u32[]{:S(2)}) collective-permute-start(bf16[1024,1792]{1,0:T(8,128)(2,1)} %collective-permute-done.10), channel_id=1, source_target_pairs={{1,0},{2,3},{5,4},{6,7},{9,8},{10,11},{13,12},{14,15},{17,16},{18,... | collective-permute-start | bytes 11010056 | tf_op jit(solution)/shard_map/ppermute | solution.py:52
  313.0 450.9 %all-reduce.5.cloned.1.call-start = ((), (), s32[]{:S(2)}) async-start(), calls=%async_computation.5 | async-start | bytes 262144 | tf_op jit(solution)/shard_map/psum | solution.py:140
  313.0 178.9 %copy-start.12 = (bf16[1024,1,2048]{0,2,1:T(8,128)(2,1)S(1)}, bf16[1024,1,2048]{0,2,1:T(8,128)(2,1)}, u32[]{:S(2)}) copy-start(bf16[1024,1,2048]{0,2,1:T(8,128)(2,1)} %all-gather.15.cloned.1.call-done) | copy-start | bytes 12582916
  328.4 308.2 %collective-permute-start.4 = (bf16[1024,1792]{1,0:T(8,128)(2,1)}, bf16[1024,1792]{1,0:T(8,128)(2,1)}, u32[]{:S(2)}, u32[]{:S(2)}) collective-permute-start(bf16[1024,1792]{1,0:T(8,128)(2,1)} %fusion.35), channel_id=1, source_target_pairs={{0,1},{3,2},{4,5},{7,6},{8,9},{11,10},{12,13},{15,14},{16,17},{19,... | collective-permute-start | bytes 11010056 | tf_op jit(solution)/shard_map/ppermute | solution.py:102
  513.6 140.6 %collective-permute-start.2 = (bf16[1024,1792]{1,0:T(8,128)(2,1)}, bf16[1024,1792]{1,0:T(8,128)(2,1)}, u32[]{:S(2)}, u32[]{:S(2)}) collective-permute-start(bf16[1024,1792]{1,0:T(8,128)(2,1)} %fusion.34), channel_id=1, source_target_pairs={{0,1},{3,2},{4,5},{7,6},{8,9},{11,10},{12,13},{15,14},{16,17},{19,... | collective-permute-start | bytes 11010056 | tf_op jit(solution)/shard_map/ppermute | solution.py:102
  682.7 1.6 copy-start.2
  682.7 2.0 copy-start.4
  682.8 6.0 copy-start.11
  684.4 5.0 copy-start.3
  684.8 4.6 slice-start
  688.8 93.3 %copy-start.1 = (bf16[1024,1024]{1,0:T(8,128)(2,1)S(1)}, bf16[1024,1024]{1,0:T(8,128)(2,1)}, u32[]{:S(2)}) copy-start(bf16[1024,1024]{1,0:T(8,128)(2,1)} %param.11) | copy-start | bytes 6291460
  766.0 16.1 %copy-start.9 = (f32[4,8192]{1,0:T(4,128)}, f32[4,8192]{1,0:T(4,128)S(1)}, u32[]{:S(2)}) copy-start(f32[4,8192]{1,0:T(4,128)S(1)} %get-tuple-element.9) | copy-start | bytes 393220
Sparse Core Ops, SparseCore 0:
  25.3 55.6 all-reduce.2
  105.0 104.9 all-gather.10
  217.1 35.9 all-gather.14
  254.8 37.4 all-gather.16
  294.0 37.4 all-gather.18
  333.2 164.5 all-gather.12
  710.7 53.1 all-reduce.4
